TPU v7x, 128 devices: a whole 4x4x4 slice. The times are simulated.
128 devices in a mesh: dp: 64 (over z, x, y_hi, core), rep: 2 (over y_lo).
Axes of the slice: x: 4, y: 4 (y_hi: 2, y_lo: 2; y = y_hi * 2 + y_lo), z: 4, core: 2. Of those that a mesh axis runs over, the one named last changes fastest.
Arguments:
- tokens: bfloat16 [200704, 1024], P(('dp', 'rep')), may hold values from -24 to 24
- cotangent: bfloat16 [200704, 2048], P(('dp', 'rep')), may hold values from -0.013671875 to 0.013671875
- global_tokens: bfloat16 [100352, 1024], P(('dp', 'rep')), may hold values from -6 to 6
- master: float32 [1024, 2048], P('dp'), may hold values from -0.1875 to 0.1875
- first_moment: float32 [1024, 2048], P('dp'), may hold values from -3 to 3
- second_moment: float32 [1024, 2048], P('dp'), may hold values from 0.05 to 2
- teacher: float32 [1024, 2048], P('dp'), may hold values from -0.1875 to 0.1875
Outputs:
- grad_input: bfloat16 [200704, 1024], P(('dp', 'rep'))
- teacher_hidden: bfloat16 [100352, 2048], P(('dp', 'rep'))
- new_master: float32 [1024, 2048], P('dp')
- new_first: float32 [1024, 2048], P('dp')
- new_second: float32 [1024, 2048], P('dp')
- new_teacher: float32 [1024, 2048], P('dp')
All inputs are finite; a program needn't handle non-finite values.
Results may differ from a plain program's by a relative error of at most 0.0065.
Values may be sent and summed in bfloat16 or wider, within the bound.
No kernel may reach another device: no remote copies, remote signals or barrier semaphores. Data moves between devices by JAX's collectives and lax.ppermute only.
A program may use at most 128 MiB of HBM per device.

v0:
```python
import math

import jax
import jax.numpy as jnp
from jax import lax
from jax.sharding import PartitionSpec as P

beta_one = 0.9
beta_two = 0.999
learn_rate = 0.001
decay_rate = 0.04
ema_momentum = 0.996
adam_epsilon = 1e-08
norm_epsilon = 1e-06
bias_one = 0.9999734386011124
bias_two = 0.09520785288629038


def layer_norm(block_tokens):
    values = block_tokens.astype(jnp.float32)
    middle = jnp.mean(values, axis=-1, keepdims=True)
    centred = values - middle
    inv_std = lax.rsqrt(jnp.mean(centred * centred, axis=-1, keepdims=True) + norm_epsilon)
    return (centred * inv_std, inv_std)


def gelu_parts(preact):
    cumul = 0.5 * (1.0 + lax.erf(preact * (1.0 / math.sqrt(2.0))))
    slope = cumul + preact * jnp.exp(-0.5 * preact * preact) * (1.0 / math.sqrt(2.0 * math.pi))
    return (preact * cumul, slope)


def adamw_update(gradient, master_rows, first_rows, second_rows, teacher_rows):
    new_first = beta_one * first_rows + (1.0 - beta_one) * gradient
    new_second = beta_two * second_rows + (1.0 - beta_two) * gradient * gradient
    update = new_first / bias_one / (jnp.sqrt(new_second / bias_two) + adam_epsilon)
    new_master = master_rows - learn_rate * (update + decay_rate * master_rows)
    new_teacher = ema_momentum * teacher_rows + (1.0 - ema_momentum) * new_master
    return (new_master, new_first, new_second, new_teacher)


def per_device(tokens, cotangent, global_tokens, master, first_moment, second_moment, teacher):
    student_local = master.astype(jnp.bfloat16)
    student_weights = lax.all_gather(student_local, "dp", axis=0, tiled=True)
    centred, inv_std = layer_norm(tokens)
    normed = centred.astype(jnp.bfloat16)
    preact = jnp.dot(normed, student_weights, preferred_element_type=jnp.float32)
    unused, slope = gelu_parts(preact)
    delta = (cotangent.astype(jnp.float32) * slope).astype(jnp.bfloat16)
    back_normed = lax.dot_general(
        delta, student_weights, (((1,), (1,)), ((), ())), preferred_element_type=jnp.float32
    )
    mean_back = jnp.mean(back_normed, axis=-1, keepdims=True)
    mean_cross = jnp.mean(back_normed * centred, axis=-1, keepdims=True)
    grad_input = (inv_std * (back_normed - mean_back - centred * mean_cross)).astype(jnp.bfloat16)
    teacher_centred, unused_std = layer_norm(global_tokens)
    teacher_normed = teacher_centred.astype(jnp.bfloat16)
    columns = teacher_normed
    teacher_pre = jnp.dot(
        columns,
        lax.all_gather(teacher.astype(jnp.bfloat16), "dp", axis=0, tiled=True),
        preferred_element_type=jnp.float32,
    )
    activated, unused_slope = gelu_parts(teacher_pre)
    teacher_hidden = activated.astype(jnp.bfloat16)
    columns = normed
    group_sum = lax.psum_scatter(
        lax.dot_general(
            columns, delta, (((0,), (0,)), ((), ())), preferred_element_type=jnp.float32
        ),
        "dp",
        scatter_dimension=0,
        tiled=True,
    )
    gradient = lax.psum(group_sum.astype(jnp.bfloat16), "rep").astype(jnp.float32)
    new_master, new_first, new_second, new_teacher = adamw_update(
        gradient, master, first_moment, second_moment, teacher
    )
    return (grad_input, teacher_hidden, new_master, new_first, new_second, new_teacher)


def solution(mesh):
    return jax.shard_map(
        per_device,
        mesh=mesh,
        in_specs=(
            P(("dp", "rep"), None),
            P(("dp", "rep"), None),
            P(("dp", "rep"), None),
            P("dp", None),
            P("dp", None),
            P("dp", None),
            P("dp", None),
        ),
        out_specs=(
            P(("dp", "rep"), None),
            P(("dp", "rep"), None),
            P("dp", None),
            P("dp", None),
            P("dp", None),
            P("dp", None),
        ),
        check_vma=False,
    )
```

profile of v0, /device:TPU:1, one launch (start us, length us, event | category | flops | bytes accessed | tf_op | source)
XLA Modules:
  0.0 575.4 jit_solution(13113108824525003452)
XLA Ops:
  7.2 0.0 all-gather.3.cloned.1.call-start
  7.2 1.7 convert_element_type.39
  8.9 0.0 reduce-scatter.2.cloned.1.call-start
  9.0 2.4 convert_reduce_fusion
  11.4 2.9 fusion.15
  14.3 73.1 %all-gather.3.cloned.1.call-done = bf16[1024,2048]{1,0:T(8,128)(2,1)} async-done(((bf16[16,2048]{1,0:T(8,128)(2,1)}), bf16[1024,2048]{1,0:T(8,128)(2,1)}) %all-gather.3.cloned.1.call-update) | async-done | bytes 4194320 | tf_op jit(solution)/shard_map/all_gather | solution.py:44
  87.4 14.6 %fusion.5 = bf16[1568,2048]{1,0:T(8,128)(2,1)S(1)} fusion(bf16[1568,2048]{1,0:T(8,128)(2,1)} %param.8, bf16[1024,2048]{1,0:T(8,128)(2,1)} %all-gather.3.cloned.1.call-done, bf16[1568,1024]{1,0:T(8,128)(2,1)S(1)} %copy-done, f32[1568]{0:T(1024)S(1)} %add_rsqrt_fusion, f32[1568]{0:T(1024)S(1)} %broadcast_multiply_fusion.2), kind=kOutput, calls=%fused_computation.6 | convolution fusion | flops 6618415104 | bytes 20263168 | tf_op jit(solution)/shard_map/dot_general | solution.py:47
  102.1 2.7 copy-done.3
  104.8 10.7 %fusion.28 = f32[1024,2048]{1,0:T(8,128)} fusion(bf16[1568,2048]{1,0:T(8,128)(2,1)S(1)} %fusion.5, bf16[1568,1024]{1,0:T(8,128)(2,1)S(1)} %copy-done, f32[1568]{0:T(1024)S(1)} %add_rsqrt_fusion, f32[1568]{0:T(1024)S(1)} %broadcast_multiply_fusion.2), kind=kOutput, calls=%fused_computation.41 | convolution fusion | flops 6583091200 | bytes 18034944 | tf_op jit(solution)/shard_map/dot_general | solution.py:68
  115.5 0.0 reduce-scatter.2.cloned.1.call-update
  115.6 0.0 all-reduce.2.cloned.1.call-start
  115.6 336.2 %reduce-scatter.2.cloned.1.call-done = f32[16,2048]{1,0:T(8,128)} async-done(((f32[1024,2048]{1,0:T(8,128)}), f32[16,2048]{1,0:T(8,128)}) %reduce-scatter.2.cloned.1.call-update) | async-done | bytes 131088 | tf_op jit(solution)/shard_map/reduce_scatter | solution.py:67
  451.9 1.5 convert_element_type.46
  453.4 0.0 all-reduce.2.cloned.1.call-update
  453.4 0.2 all-gather.5.cloned.1.call-start
  453.6 29.7 %all-reduce.2.cloned.1.call-done = bf16[16,2048]{1,0:T(8,128)(2,1)} async-done(((bf16[16,2048]{1,0:T(8,128)(2,1)}), bf16[16,2048]{1,0:T(8,128)(2,1)}) %all-reduce.2.cloned.1.call-update) | async-done | bytes 65552 | tf_op jit(solution)/shard_map/psum | solution.py:75
  483.4 1.9 multiply_add_fusion
  485.3 0.0 all-gather.5.cloned.1.call-update
  485.3 1.7 convert_reduce_fusion.1
  487.0 2.0 fusion.18
  489.0 14.0 %fusion.34 = (f32[1568]{0:T(1024)S(1)}, f32[1568]{0:T(1024)S(1)}, f32[1568,1024]{1,0:T(8,128)S(1)}) fusion(f32[1568]{0:T(1024)S(1)} %add_rsqrt_fusion, f32[1568]{0:T(1024)S(1)} %broadcast_multiply_fusion.2, bf16[1568,1024]{1,0:T(8,128)(2,1)S(1)} %copy-done, bf16[1568,2048]{1,0:T(8,128)(2,1)} %copy-done.3, bf16[1024,2048]{1,0:T(8,128)(2,1)} %all-gather.3.cloned.1.call-done), kind=kOutput, calls=%fused_computation.43 | convolution fusion | flops 6586299392 | bytes 20275712 | tf_op jit(solution)/shard_map/dot_general | solution.py:50
  503.1 3.0 fusion.14
  506.1 54.7 %all-gather.5.cloned.1.call-done = bf16[1024,2048]{1,0:T(8,128)(2,1)} async-done(((bf16[16,2048]{1,0:T(8,128)(2,1)}), bf16[1024,2048]{1,0:T(8,128)(2,1)}) %all-gather.5.cloned.1.call-update) | async-done | bytes 4194320 | tf_op jit(solution)/shard_map/all_gather | solution.py:61
  560.8 8.0 %multiply_convert_fusion = bf16[784,2048]{1,0:T(8,128)(2,1)} fusion(bf16[1024,2048]{1,0:T(8,128)(2,1)} %all-gather.5.cloned.1.call-done, bf16[784,1024]{1,0:T(8,128)(2,1)} %param.9, f32[784]{0:T(1024)S(1)} %add_rsqrt_fusion.1, f32[784]{0:T(1024)S(1)} %broadcast_multiply_fusion.3), kind=kOutput, calls=%fused_computation.19 | convolution fusion | flops 3299573760 | bytes 9017472 | tf_op jit(solution)/shard_map/dot_general | solution.py:59
  (13 shorter events, 0.1 us)
Async XLA Ops:
  7.2 80.3 %copy-start = (bf16[1568,1024]{1,0:T(8,128)(2,1)S(1)}, bf16[1568,1024]{1,0:T(8,128)(2,1)}, u32[]{:S(2)}) copy-start(bf16[1568,1024]{1,0:T(8,128)(2,1)} %param.7) | copy-start | bytes 9633796
  7.2 80.3 %all-gather.3.cloned.1.call-start = ((), (), s32[]{:S(2)}) async-start(), calls=%async_computation.1 | async-start | bytes 4259840 | tf_op jit(solution)/shard_map/all_gather | solution.py:44
  8.9 442.9 %reduce-scatter.2.cloned.1.call-start = ((), (), s32[]{:S(2)}) async-start(), calls=%async_computation.3 | async-start | bytes 8519680 | tf_op jit(solution)/shard_map/reduce_scatter | solution.py:67
  102.1 2.7 copy-start.3
  115.5 367.8 %copy-start.1 = (f32[16,2048]{1,0:T(8,128)S(1)}, f32[16,2048]{1,0:T(8,128)}, u32[]{:S(2)}) copy-start(f32[16,2048]{1,0:T(8,128)} %param.10) | copy-start | bytes 393220
  115.5 367.8 %copy-start.2 = (f32[16,2048]{1,0:T(8,128)S(1)}, f32[16,2048]{1,0:T(8,128)}, u32[]{:S(2)}) copy-start(f32[16,2048]{1,0:T(8,128)} %param.13) | copy-start | bytes 393220
  115.6 367.8 %all-reduce.2.cloned.1.call-start = ((), (), s32[]{:S(2)}) async-start(), calls=%async_computation.4 | async-start | bytes 131072 | tf_op jit(solution)/shard_map/psum | solution.py:75
  453.4 107.4 %all-gather.5.cloned.1.call-start = ((), (), s32[]{:S(2)}) async-start(), calls=%async_computation.2 | async-start | bytes 4259840 | tf_op jit(solution)/shard_map/all_gather | solution.py:61
Sparse Core Ops, SparseCore 0:
  11.7 75.6 all-gather.2
  115.7 336.1 reduce-scatter.1
  454.8 28.4 all-reduce.1
  486.9 73.8 all-gather.4
where the time goes:
time: 576 us; the launch traced here: 575 us
  waiting for transfers between devices  494 us (86%)
  matrix products  47.4 us (8%)
  other arithmetic  17.2 us (3%)
  between operations  13.8 us (2%)
    reduce_scatter x1, waiting for transfers between devices, per_device(): lax.psum_scatter(lax.dot_general(columns, delta, (((0,), (0,)), ((), ()))...  336 us
    all_gather x1, waiting for transfers between devices, per_device(): student_weights = lax.all_gather(student_local, 'dp', axis=0, tiled=True)  73.1 us
    all_gather x1, waiting for transfers between devices, per_device(): lax.all_gather(teacher.astype(jnp.bfloat16), 'dp', axis=0, tiled=True)  54.7 us
    psum x1, waiting for transfers between devices, per_device(): lax.psum(group_sum.astype(jnp.bfloat16), 'rep').astype(jnp.float32)  29.7 us
    dot_general x1, matrix products, per_device(): jnp.dot(normed, student_weights, preferred_element_type=jnp.float32)  14.6 us
    dot_general x1, matrix products, per_device(): lax.dot_general(delta, student_weights, (((1,), (1,)), ((), ())), preferr...  14 us
  transfers between devices with their start and end apart: 4, of which 4 were waited for; matrix products, arithmetic and copies ran while one was open for 5% of the time, Pallas kernels for 0%

commit v1 on v0

v1 whole, which is shorter than its diff:
```python
import math

import jax
import jax.numpy as jnp
from jax import lax
from jax.sharding import Mesh
from jax.sharding import PartitionSpec as P

beta_one = 0.9
beta_two = 0.999
learn_rate = 0.001
decay_rate = 0.04
ema_momentum = 0.996
adam_epsilon = 1e-08
norm_epsilon = 1e-06
bias_one = 0.9999734386011124
bias_two = 0.09520785288629038

CHIPS = ("z", "x", "yh")
SWAP = [(0, 1), (1, 0)]
bf16, f32 = jnp.bfloat16, jnp.float32


def layer_norm(block_tokens):
    values = block_tokens.astype(f32)
    middle = jnp.mean(values, axis=-1, keepdims=True)
    centred = values - middle
    inv_std = lax.rsqrt(jnp.mean(centred * centred, axis=-1, keepdims=True) + norm_epsilon)
    return (centred * inv_std, inv_std)


def gelu_parts(preact):
    cumul = 0.5 * (1.0 + lax.erf(preact * (1.0 / math.sqrt(2.0))))
    slope = cumul + preact * jnp.exp(-0.5 * preact * preact) * (1.0 / math.sqrt(2.0 * math.pi))
    return (preact * cumul, slope)


def adamw_update(gradient, master_rows, first_rows, second_rows, teacher_rows):
    new_first = beta_one * first_rows + (1.0 - beta_one) * gradient
    new_second = beta_two * second_rows + (1.0 - beta_two) * gradient * gradient
    update = new_first / bias_one / (jnp.sqrt(new_second / bias_two) + adam_epsilon)
    new_master = master_rows - learn_rate * (update + decay_rate * master_rows)
    new_teacher = ema_momentum * teacher_rows + (1.0 - ema_momentum) * new_master
    return (new_master, new_first, new_second, new_teacher)


def swap(block):
    return lax.ppermute(block, "core", SWAP)


def in_core_order(mine, theirs, axis):
    first = lax.axis_index("core") == 0
    return jnp.where(
        first,
        jnp.concatenate([mine, theirs], axis=axis),
        jnp.concatenate([theirs, mine], axis=axis),
    )


def columns_of(array, core):
    half = array.shape[1] // 2
    return lax.dynamic_slice_in_dim(array, core * half, half, axis=1)


def per_device(tokens, cotangent, global_tokens, master, first_moment, second_moment, teacher):
    core = lax.axis_index("core")
    teacher_weights = lax.all_gather(
        teacher.astype(bf16), ("z", "x", "yh", "core"), axis=0, tiled=True
    )

    rounded = master.astype(bf16)
    theirs = swap(columns_of(rounded, 1 - core))
    block = in_core_order(columns_of(rounded, core), theirs, 0)
    copies = jnp.broadcast_to(block[None], (32,) + block.shape).reshape(-1, block.shape[1])
    weights_own = lax.all_to_all(copies, CHIPS, 0, 0, tiled=True)
    weights_other = swap(weights_own)

    centred, inv_std = layer_norm(tokens)
    normed = centred.astype(bf16)

    def delta_of(weights, which):
        preact = jnp.dot(normed, weights, preferred_element_type=f32)
        unused, slope = gelu_parts(preact)
        return (columns_of(cotangent, which).astype(f32) * slope).astype(bf16)

    def gradient_of(delta):
        return lax.dot_general(normed, delta, (((0,), (0,)), ((), ())), preferred_element_type=f32)

    delta_own = delta_of(weights_own, core)
    delta_other = delta_of(weights_other, 1 - core)
    sent = swap(gradient_of(delta_other).astype(bf16))
    partial = (gradient_of(delta_own) + sent.astype(f32)).astype(bf16)
    pieces = lax.all_to_all(partial, CHIPS, 0, 0, tiled=True)
    group = jnp.sum(pieces.reshape(32, 32, -1).astype(f32), axis=0)
    group = lax.optimization_barrier(group.astype(bf16))
    group = group.astype(f32) + lax.ppermute(group, "yl", SWAP).astype(f32)
    mine = lax.dynamic_slice_in_dim(group, core * 16, 16, axis=0)
    other = lax.dynamic_slice_in_dim(group, (1 - core) * 16, 16, axis=0)
    gradient = in_core_order(mine, swap(other), 1)
    new_master, new_first, new_second, new_teacher = adamw_update(
        gradient, master, first_moment, second_moment, teacher
    )

    back = lax.dot_general(
        delta_own, weights_own, (((1,), (1,)), ((), ())), preferred_element_type=f32
    ) + lax.dot_general(
        delta_other, weights_other, (((1,), (1,)), ((), ())), preferred_element_type=f32
    )
    mean_back = jnp.mean(back, axis=-1, keepdims=True)
    mean_cross = jnp.mean(back * centred, axis=-1, keepdims=True)
    grad_input = (inv_std * (back - mean_back - centred * mean_cross)).astype(bf16)

    teacher_centred, unused_std = layer_norm(global_tokens)
    teacher_pre = jnp.dot(
        teacher_centred.astype(bf16), teacher_weights, preferred_element_type=f32
    )
    activated, unused_slope = gelu_parts(teacher_pre)
    return (grad_input, activated.astype(bf16), new_master, new_first, new_second, new_teacher)


def solution(mesh):
    split = Mesh(mesh.devices.reshape(4, 4, 2, 2, 2), ("z", "x", "yh", "core", "yl"))
    tokens = P(("z", "x", "yh", "core", "yl"), None)
    rows = P(("z", "x", "yh", "core"), None)
    return jax.shard_map(
        per_device,
        mesh=split,
        in_specs=(tokens, tokens, tokens, rows, rows, rows, rows),
        out_specs=(tokens, tokens, rows, rows, rows, rows),
        check_vma=False,
    )
```

time: 576 us -> 210 us (0.36)
  waiting for transfers between devices: 494 us -> 57.4 us
  blocking collectives: 0 us -> 74.5 us
  starting transfers between devices: 0.35 us -> 6.83 us
    reduce_scatter x1 -> x0, waiting for transfers between devices: 336 us -> none  [per_device(): lax.psum_scatter(lax.dot_general(columns, delta, (((0,), (0,)), ((), ()))...]
    all_gather x2 -> x1, waiting for transfers between devices: 128 us -> 50.5 us  [per_device(): lax.all_gather(teacher.astype(bf16), ('z', 'x', 'yh', 'core'), axis=0, ti...]
    all_to_all x0 -> x2, blocking collectives: none -> 74.5 us  [the longest x1 40.4 us: per_device(): weights_own = lax.all_to_all(copies, CHIPS, 0, 0, tiled=True)]
    psum x1 -> x0, waiting for transfers between devices: 29.7 us -> none  [per_device(): lax.psum(group_sum.astype(jnp.bfloat16), 'rep').astype(jnp.float32)]
    ppermute x0 -> x5, waiting for transfers between devices: none -> 6.89 us  [the longest x4 4.01 us: swap(): return lax.ppermute(block, 'core', SWAP)]
    ppermute x0 -> x5, starting transfers between devices: none -> 6.8 us  [the longest x4 6.38 us: swap(): return lax.ppermute(block, 'core', SWAP)]
    dot_general x4 -> x7, matrix products: 47.4 us -> 42.7 us  [the longest x2 15 us: delta_of(): preact = jnp.dot(normed, weights, preferred_element_type=f32)]
  transfers between devices with their start and end apart: 4 -> 6, of which waited for: 4 -> 5; matrix products, arithmetic and copies ran while one was open for 5% -> 13% of each run, Pallas kernels for 0% -> 0%
where the time goes in v1:
time: 210 us
  blocking collectives  74.5 us (35%)
  waiting for transfers between devices  57.4 us (27%)
  matrix products  42.7 us (20%)
  between operations  14.2 us (7%)
  other arithmetic  14 us (7%)
  starting transfers between devices  6.83 us (3%)
    all_gather x1, waiting for transfers between devices, per_device(): lax.all_gather(teacher.astype(bf16), ('z', 'x', 'yh', 'core'), axis=0, ti...  50.5 us
    all_to_all x1, blocking collectives, per_device(): weights_own = lax.all_to_all(copies, CHIPS, 0, 0, tiled=True)  40.4 us
    all_to_all x1, blocking collectives, per_device(): pieces = lax.all_to_all(partial, CHIPS, 0, 0, tiled=True)  34.1 us
    dot_general x2, matrix products, delta_of(): preact = jnp.dot(normed, weights, preferred_element_type=f32)  15 us
    dot_general x2, matrix products, gradient_of(): lax.dot_general(normed, delta, (((0,), (0,)), ((), ())), preferred_elemen...  9.04 us
    dot_general x1, matrix products, per_device(): jnp.dot(teacher_centred.astype(bf16), teacher_weights, preferred_element_...  8.03 us
    ppermute x4, starting transfers between devices, swap(): return lax.ppermute(block, 'core', SWAP)  6.38 us
    dot_general x1, matrix products, per_device(): lax.dot_general(delta_own, weights_own, (((1,), (1,)), ((), ())), preferr...  6.28 us
  transfers between devices with their start and end apart: 6, of which 5 were waited for; matrix products, arithmetic and copies ran while one was open for 13% of the time, Pallas kernels for 0%

profile of v1, /device:TPU:1, one launch (start us, length us, event | category | flops | bytes accessed | tf_op | source)
XLA Modules:
  0.0 210.0 jit_solution(1945338460343846266)
XLA Ops:
  7.2 1.1 convert_element_type.56
  8.3 1.5 collective-permute-start
  9.8 0.9 collective-permute-done
  10.9 40.4 %all_to_all.18 = bf16[32,32,1024]{2,1,0:T(8,128)(2,1)S(1)} all-to-all(bf16[32,32,1024]{2,1,0:T(8,128)(2,1)S(1)} %broadcast_in_dim.2), channel_id=1, replica_groups=mesh['z'=4,'x'=4,'yh'=2,'core'=2,'yl'=2] {'z','x','yh'}, dimensions={0} | all-to-all | bytes 4194304 | tf_op jit(solution)/shard_map/all_to_all | solution.py:75
  51.4 1.8 collective-permute-start.1
  53.7 1.0 fusion.9
  54.7 2.2 %collective-permute-done.1 = bf16[1024,1024]{1,0:T(8,128)(2,1)S(1)} collective-permute-done((bf16[1024,1024]{1,0:T(8,128)(2,1)S(1)}, bf16[1024,1024]{1,0:T(8,128)(2,1)S(1)}, u32[]{:S(2)}, u32[]{:S(2)}) %collective-permute-start.1) | collective-permute-done | bytes 2097184 | tf_op jit(solution)/shard_map/ppermute | solution.py:48
  56.9 7.5 %fusion.21 = bf16[1568,1024]{1,0:T(8,128)(2,1)S(1)} fusion(bf16[1568,2048]{1,0:T(8,128)(2,1)S(1)} %copy-done.4, s32[]{:T(128)S(6)} %select_n.36, bf16[1024,1024]{1,0:T(8,128)(2,1)S(1)} %collective-permute-done.1, bf16[1568,1024]{1,0:T(8,128)(2,1)S(1)} %copy-done, f32[1568]{0:T(1024)S(1)} %add_rsqrt_fusion, f32[1568]{0:T(1024)S(1)} %broadcast_multiply_fusion.2), kind=kOutput, calls=%fused_computation.25 | convolution fusion | flops 3312418816 | bytes 11743492 | tf_op jit(solution)/shard_map/dot_general | solution.py:82
  64.5 4.5 %convolution_convert_fusion = bf16[1024,1024]{1,0:T(8,128)(2,1)S(1)} fusion(bf16[1568,1024]{1,0:T(8,128)(2,1)S(1)} %fusion.21, bf16[1568,1024]{1,0:T(8,128)(2,1)S(1)} %copy-done, f32[1568]{0:T(1024)S(1)} %add_rsqrt_fusion, f32[1568]{0:T(1024)S(1)} %broadcast_multiply_fusion.2), kind=kOutput, calls=%fused_computation.35 | convolution fusion | flops 3295805440 | bytes 8532224 | tf_op jit(solution)/shard_map/dot_general | solution.py:87
  69.4 7.5 %fusion.15 = bf16[1568,1024]{1,0:T(8,128)(2,1)S(1)} fusion(bf16[1568,2048]{1,0:T(8,128)(2,1)S(1)} %copy-done.4, s32[]{:T(128)S(6)} %select_n.34, bf16[1024,1024]{1,0:T(8,128)(2,1)S(1)} %bitcast.12, bf16[1568,1024]{1,0:T(8,128)(2,1)S(1)} %copy-done, f32[1568]{0:T(1024)S(1)} %add_rsqrt_fusion, f32[1568]{0:T(1024)S(1)} %broadcast_multiply_fusion.2), kind=kOutput, calls=%fused_computation.19 | convolution fusion | flops 3312418816 | bytes 11743492 | tf_op jit(solution)/shard_map/dot_general | solution.py:82
  76.9 4.5 %add_convert_fusion = bf16[1024,1024]{1,0:T(8,128)(2,1)S(1)} fusion(bf16[1024,1024]{1,0:T(8,128)(2,1)S(1)} %collective-permute-done.2, bf16[1568,1024]{1,0:T(8,128)(2,1)S(1)} %fusion.15, bf16[1568,1024]{1,0:T(8,128)(2,1)S(1)} %copy-done, f32[1568]{0:T(1024)S(1)} %add_rsqrt_fusion, f32[1568]{0:T(1024)S(1)} %broadcast_multiply_fusion.2), kind=kOutput, calls=%fused_computation.27 | convolution fusion | flops 3297902592 | bytes 10629376 | tf_op jit(solution)/shard_map/dot_general | solution.py:87
  81.5 34.1 %all_to_all.19 = bf16[32,32,1024]{2,1,0:T(8,128)(2,1)} all-to-all(bf16[32,32,1024]{2,1,0:T(8,128)(2,1)S(1)} %bitcast.14), channel_id=1, replica_groups=mesh['z'=4,'x'=4,'yh'=2,'core'=2,'yl'=2] {'z','x','yh'}, dimensions={0} | all-to-all | bytes 4194304 | tf_op jit(solution)/shard_map/all_to_all | solution.py:93
  115.6 2.0 reduce_sum.72
  118.0 2.9 %collective-permute-done.3 = bf16[32,1024]{1,0:T(8,128)(2,1)} collective-permute-done((bf16[32,1024]{1,0:T(8,128)(2,1)S(1)}, bf16[32,1024]{1,0:T(8,128)(2,1)}, u32[]{:S(2)}, u32[]{:S(2)}) %collective-permute-start.3) | collective-permute-done | bytes 65568 | tf_op jit(solution)/shard_map/ppermute | solution.py:96
  121.7 2.7 %collective-permute-start.4 = (f32[16,1024]{1,0:T(8,128)S(1)}, f32[16,1024]{1,0:T(8,128)S(1)}, u32[]{:S(2)}, u32[]{:S(2)}) collective-permute-start(f32[16,1024]{1,0:T(8,128)S(1)} %get-tuple-element.13), channel_id=1, source_target_pairs={{0,2},{2,0},{1,3},{3,1},{4,6},{6,4},{5,7},{7,5},{8,10},{10,8},{9,1... | collective-permute-start | bytes 196616 | tf_op jit(solution)/shard_map/ppermute | solution.py:48
  124.4 0.9 collective-permute-done.4
  125.3 1.8 multiply_add_fusion
  127.2 1.7 convert_reduce_fusion.1
  128.9 2.0 fusion.24
  130.9 6.3 %fusion.48 = f32[1568,1024]{1,0:T(8,128)S(1)} fusion(bf16[1568,1024]{1,0:T(8,128)(2,1)} %copy-done.9, bf16[1024,1024]{1,0:T(8,128)(2,1)} %bitcast.13), kind=kOutput, calls=%fused_computation.61 | convolution fusion | flops 3288334336 | bytes 11730944 | tf_op jit(solution)/shard_map/dot_general | solution.py:104
  137.2 4.3 %fusion.46 = (f32[1568]{0:T(1024)S(1)}, f32[1568]{0:T(1024)S(1)}, f32[1568,1024]{1,0:T(8,128)S(1)}) fusion(f32[1568]{0:T(1024)S(1)} %add_rsqrt_fusion, f32[1568]{0:T(1024)S(1)} %broadcast_multiply_fusion.2, bf16[1568,1024]{1,0:T(8,128)(2,1)S(1)} %copy-done, f32[1568,1024]{1,0:T(8,128)S(1)} %fusion.48, bf16[1568,1024]{1,0:T(8,128)(2,1)S(1)} %copy-done.8, ...), kind=kOutput, calls=%fused_computation.60 | convolution fusion | flops 3299570688 | bytes 21389824 | tf_op jit(solution)/shard_map/dot_general | solution.py:106
  141.6 3.0 %fusion.8 = bf16[1568,1024]{1,0:T(8,128)(2,1)} fusion(bf16[1568,1024]{1,0:T(8,128)(2,1)S(1)} %copy-done, f32[1568,1024]{1,0:T(8,128)S(1)} %get-tuple-element.17, f32[1568]{0:T(1024)S(1)} %get-tuple-element.18, f32[1568]{0:T(1024)S(1)} %get-tuple-element.19, f32[1568]{0:T(1024)S(1)} %add_rsqrt_fusion, f32[1568]{0:T(1024)S(1)} %broadcast_multiply_fusion.2), kind=kLoop, calls=%fused_computation.12 | loop fusion | flops 12845056 | bytes 12870144 | tf_op jit(solution)/shard_map/convert_element_type | solution.py:111
  144.6 50.5 %all-gather.2.cloned.1.call-done = bf16[1024,2048]{1,0:T(8,128)(2,1)} async-done(((bf16[16,2048]{1,0:T(8,128)(2,1)}), bf16[1024,2048]{1,0:T(8,128)(2,1)}) %all-gather.2.cloned.1.call-update) | async-done | bytes 4194320 | tf_op jit(solution)/shard_map/all_gather | solution.py:67
  195.1 8.0 %multiply_convert_fusion = bf16[784,2048]{1,0:T(8,128)(2,1)} fusion(bf16[1024,2048]{1,0:T(8,128)(2,1)} %all-gather.2.cloned.1.call-done, bf16[784,1024]{1,0:T(8,128)(2,1)} %param.9, f32[784]{0:T(1024)S(1)} %add_rsqrt_fusion.1, f32[784]{0:T(1024)S(1)} %broadcast_multiply_fusion.3), kind=kOutput, calls=%fused_computation.26 | convolution fusion | flops 3299573760 | bytes 9017472 | tf_op jit(solution)/shard_map/dot_general | solution.py:114
  (36 shorter events, 2.6 us)
Async XLA Ops:
  7.2 46.0 %copy-start = (bf16[1568,1024]{1,0:T(8,128)(2,1)S(1)}, bf16[1568,1024]{1,0:T(8,128)(2,1)}, u32[]{:S(2)}) copy-start(bf16[1568,1024]{1,0:T(8,128)(2,1)} %param.7) | copy-start | bytes 9633796
  7.2 187.9 %all-gather.2.cloned.1.call-start = ((), (), s32[]{:S(2)}) async-start(), calls=%async_computation.2 | async-start | bytes 4259840 | tf_op jit(solution)/shard_map/all_gather | solution.py:67
  8.3 2.4 %collective-permute-start = (bf16[16,1024]{1,0:T(8,128)(2,1)S(1)}, bf16[16,1024]{1,0:T(8,128)(2,1)S(1)}, u32[]{:S(2)}, u32[]{:S(2)}) collective-permute-start(bf16[16,1024]{1,0:T(8,128)(2,1)S(1)} %get-tuple-element.16), channel_id=1, source_target_pairs={{0,2},{2,0},{1,3},{3,1},{4,6},{6,4},{5,7},{7,5},{8,10},{10,8},{9,1... | collective-permute-start | bytes 98312 | tf_op jit(solution)/shard_map/ppermute | solution.py:48
  10.7 46.3 %copy-start.4 = (bf16[1568,2048]{1,0:T(8,128)(2,1)S(1)}, bf16[1568,2048]{1,0:T(8,128)(2,1)}, u32[]{:S(2)}) copy-start(bf16[1568,2048]{1,0:T(8,128)(2,1)} %param.8) | copy-start | bytes 19267588
  51.4 18.1 %copy-start.1 = (bf16[32,32,1024]{2,1,0:T(8,128)(2,1)}, bf16[32,32,1024]{2,1,0:T(8,128)(2,1)S(1)}, u32[]{:S(2)}) copy-start(bf16[32,32,1024]{2,1,0:T(8,128)(2,1)S(1)} %all_to_all.18) | copy-start | bytes 6291460
  51.4 5.6 %collective-permute-start.1 = (bf16[1024,1024]{1,0:T(8,128)(2,1)S(1)}, bf16[1024,1024]{1,0:T(8,128)(2,1)S(1)}, u32[]{:S(2)}, u32[]{:S(2)}) collective-permute-start(bf16[1024,1024]{1,0:T(8,128)(2,1)S(1)} %bitcast.11), channel_id=1, source_target_pairs={{0,2},{2,0},{1,3},{3,1},{4,6},{6,4},{5,7},{7,5},{8,10},{10,8},{9,1... | collective-permute-start | bytes 6291464 | tf_op jit(solution)/shard_map/ppermute | solution.py:48
  56.9 7.5 %copy-start.5 = (bf16[1024,1024]{1,0:T(8,128)(2,1)}, bf16[1024,1024]{1,0:T(8,128)(2,1)S(1)}, u32[]{:S(2)}) copy-start(bf16[1024,1024]{1,0:T(8,128)(2,1)S(1)} %collective-permute-done.1) | copy-start | bytes 6291460
  64.4 4.5 %copy-start.7 = (bf16[1568,1024]{1,0:T(8,128)(2,1)}, bf16[1568,1024]{1,0:T(8,128)(2,1)S(1)}, u32[]{:S(2)}) copy-start(bf16[1568,1024]{1,0:T(8,128)(2,1)S(1)} %fusion.21) | copy-start | bytes 9633796
  69.0 7.9 %collective-permute-start.2 = (bf16[1024,1024]{1,0:T(8,128)(2,1)S(1)}, bf16[1024,1024]{1,0:T(8,128)(2,1)S(1)}, u32[]{:S(2)}, u32[]{:S(2)}) collective-permute-start(bf16[1024,1024]{1,0:T(8,128)(2,1)S(1)} %convolution_convert_fusion), channel_id=1, source_target_pairs={{0,2},{2,0},{1,3},{3,1},{4,6},{6,4},{5,7},{7,5},{8,10},{10,8},{9,1... | collective-permute-start | bytes 6291464 | tf_op jit(solution)/shard_map/ppermute | solution.py:48
  76.9 4.6 %copy-start.9 = (bf16[1568,1024]{1,0:T(8,128)(2,1)}, bf16[1568,1024]{1,0:T(8,128)(2,1)S(1)}, u32[]{:S(2)}) copy-start(bf16[1568,1024]{1,0:T(8,128)(2,1)S(1)} %fusion.15) | copy-start | bytes 9633796
  81.5 43.8 %copy-start.2 = (f32[16,2048]{1,0:T(8,128)S(1)}, f32[16,2048]{1,0:T(8,128)}, u32[]{:S(2)}) copy-start(f32[16,2048]{1,0:T(8,128)} %param.10) | copy-start | bytes 393220
  81.5 43.8 %copy-start.3 = (f32[16,2048]{1,0:T(8,128)S(1)}, f32[16,2048]{1,0:T(8,128)}, u32[]{:S(2)}) copy-start(f32[16,2048]{1,0:T(8,128)} %param.13) | copy-start | bytes 393220
  117.6 3.3 %collective-permute-start.3 = (bf16[32,1024]{1,0:T(8,128)(2,1)S(1)}, bf16[32,1024]{1,0:T(8,128)(2,1)}, u32[]{:S(2)}, u32[]{:S(2)}) collective-permute-start(bf16[32,1024]{1,0:T(8,128)(2,1)S(1)} %reduce_sum.72), channel_id=1, source_target_pairs={{0,1},{1,0},{2,3},{3,2},{4,5},{5,4},{6,7},{7,6},{8,9},{9,8},{10,11... | collective-permute-start | bytes 196616 | tf_op jit(solution)/shard_map/ppermute | solution.py:96
  121.7 3.6 %collective-permute-start.4 = (f32[16,1024]{1,0:T(8,128)S(1)}, f32[16,1024]{1,0:T(8,128)S(1)}, u32[]{:S(2)}, u32[]{:S(2)}) collective-permute-start(f32[16,1024]{1,0:T(8,128)S(1)} %get-tuple-element.13), channel_id=1, source_target_pairs={{0,2},{2,0},{1,3},{3,1},{4,6},{6,4},{5,7},{7,5},{8,10},{10,8},{9,1... | collective-permute-start | bytes 196616 | tf_op jit(solution)/shard_map/ppermute | solution.py:48
  130.9 6.3 %copy-start.6 = (bf16[1024,1024]{1,0:T(8,128)(2,1)S(1)}, bf16[1024,1024]{1,0:T(8,128)(2,1)}, u32[]{:S(2)}) copy-start(bf16[1024,1024]{1,0:T(8,128)(2,1)} %copy-done.5) | copy-start | bytes 6291460
  130.9 6.3 %copy-start.8 = (bf16[1568,1024]{1,0:T(8,128)(2,1)S(1)}, bf16[1568,1024]{1,0:T(8,128)(2,1)}, u32[]{:S(2)}) copy-start(bf16[1568,1024]{1,0:T(8,128)(2,1)} %copy-done.7) | copy-start | bytes 9633796
Sparse Core Ops, SparseCore 0:
  127.3 67.7 all-gather.1

commit v2 on v1

v2 whole, which is shorter than its diff:
```python
import math

import jax
import jax.numpy as jnp
from jax import lax
from jax.experimental import pallas as pl
from jax.experimental.pallas import tpu as pltpu
from jax.sharding import Mesh
from jax.sharding import PartitionSpec as P

beta_one = 0.9
beta_two = 0.999
learn_rate = 0.001
decay_rate = 0.04
ema_momentum = 0.996
adam_epsilon = 1e-08
norm_epsilon = 1e-06
bias_one = 0.9999734386011124
bias_two = 0.09520785288629038

SWAP = [(0, 1), (1, 0)]
ACROSS = [(0, 3), (3, 0), (1, 2), (2, 1)]
EVEN = ("zh", "xh")
STEPS = ((1, 0), (0, 1), (-1, -1))
bf16, f32 = jnp.bfloat16, jnp.float32


def params():
    return pltpu.CompilerParams(vmem_limit_bytes=48 * 1024 * 1024)


def cost(flops, bytes_accessed):
    return pl.CostEstimate(flops=flops, bytes_accessed=bytes_accessed, transcendentals=0)


def layer_norm(block_tokens):
    values = block_tokens.astype(f32)
    middle = jnp.mean(values, axis=-1, keepdims=True)
    centred = values - middle
    inv_std = lax.rsqrt(jnp.mean(centred * centred, axis=-1, keepdims=True) + norm_epsilon)
    return (centred * inv_std, inv_std)


def gelu_parts(preact):
    cumul = 0.5 * (1.0 + lax.erf(preact * (1.0 / math.sqrt(2.0))))
    slope = cumul + preact * jnp.exp(-0.5 * preact * preact) * (1.0 / math.sqrt(2.0 * math.pi))
    return (preact * cumul, slope)


def adamw_update(gradient, master_rows, first_rows, second_rows, teacher_rows):
    new_first = beta_one * first_rows + (1.0 - beta_one) * gradient
    new_second = beta_two * second_rows + (1.0 - beta_two) * gradient * gradient
    update = new_first / bias_one / (jnp.sqrt(new_second / bias_two) + adam_epsilon)
    new_master = master_rows - learn_rate * (update + decay_rate * master_rows)
    new_teacher = ema_momentum * teacher_rows + (1.0 - ema_momentum) * new_master
    return (new_master, new_first, new_second, new_teacher)


def swap(block):
    return lax.ppermute(block, "core", SWAP)


def across(block):
    return lax.ppermute(block, ("yh", "yl"), ACROSS)


def shifted(block, step, sign):
    moves = [
        (4 * z + x, 4 * ((z + sign * step[0]) % 4) + (x + sign * step[1]) % 4)
        for z in range(4)
        for x in range(4)
    ]
    return lax.ppermute(block, ("zh", "zl", "xh", "xl"), moves)


def in_order(mine, theirs, axis_name, axis):
    first = lax.axis_index(axis_name) == 0
    return jnp.where(
        first,
        jnp.concatenate([mine, theirs], axis=axis),
        jnp.concatenate([theirs, mine], axis=axis),
    )


def columns_of(array, core):
    half = array.shape[-1] // 2
    return lax.dynamic_slice_in_dim(array, core * half, half, axis=array.ndim - 1)


def even_gather(block):
    copies = jnp.broadcast_to(block[None], (4,) + block.shape)
    return lax.all_to_all(copies, EVEN, 0, 0, tiled=True)


def class_of(step):
    return (
        (lax.axis_index("zl") + step[0]) % 2,
        (lax.axis_index("xl") + step[1]) % 2,
    )


def assemble_kernel(class_ref, *refs):
    whole_ref = refs[4]
    for part_ref, (dz, dx) in zip(refs[:4], ((0, 0),) + STEPS):
        zl = lax.rem(class_ref[0] + dz % 2, 2)
        xl = lax.rem(class_ref[1] + dx % 2, 2)
        for even in range(4):
            chip = (4 * (even // 2) + 2 * zl + even % 2) * 2 + xl
            whole_ref[pl.ds(pl.multiple_of(64 * chip, 64), 64), :] = part_ref[even]


def assemble(parts):
    parity = jnp.stack([lax.axis_index("zl"), lax.axis_index("xl")]).astype(jnp.int32)
    half = parts[0].shape[-1]
    tile = half // 2
    piece = pl.BlockSpec((4, 64, tile), lambda i, parity: (0, 0, i))
    return pl.pallas_call(
        assemble_kernel,
        grid_spec=pltpu.PrefetchScalarGridSpec(
            num_scalar_prefetch=1,
            grid=(2,),
            in_specs=[piece] * 4,
            out_specs=pl.BlockSpec((1024, tile), lambda i, parity: (0, i)),
        ),
        out_shape=jax.ShapeDtypeStruct((1024, half), parts[0].dtype),
        compiler_params=params(),
        cost_estimate=cost(0, 4 * 1024 * half),
    )(parity, *parts)


def steps_of(part):
    return [part] + [shifted(part, step, 1) for step in STEPS]


def norm_kernel(tokens_ref, normed_ref):
    normed_ref[...] = layer_norm(tokens_ref[...])[0].astype(bf16)


def norm_call(tokens):
    rows, width = tokens.shape
    spec = pl.BlockSpec((784, width), lambda i: (i, 0))
    return pl.pallas_call(
        norm_kernel,
        grid=(rows // 784,),
        in_specs=[spec],
        out_specs=spec,
        out_shape=jax.ShapeDtypeStruct((rows, width), bf16),
        compiler_params=params(),
        cost_estimate=cost(0, 1024),
    )(tokens)


def input_kernel(delta_own_ref, delta_other_ref, own_ref, other_ref, tokens_ref, out_ref):
    dims = (((1,), (1,)), ((), ()))
    back = lax.dot_general(delta_own_ref[...], own_ref[...], dims, preferred_element_type=f32)
    back += lax.dot_general(delta_other_ref[...], other_ref[...], dims, preferred_element_type=f32)
    centred, inv_std = layer_norm(tokens_ref[...])
    mean_back = jnp.mean(back, axis=-1, keepdims=True)
    mean_cross = jnp.mean(back * centred, axis=-1, keepdims=True)
    out_ref[...] = (inv_std * (back - mean_back - centred * mean_cross)).astype(bf16)


def input_call(delta_own, delta_other, own, other, tokens):
    rows, width = tokens.shape
    half = own.shape[1]
    deltas = pl.BlockSpec((784, half), lambda i: (i, 0))
    weights = pl.BlockSpec((width, half), lambda i: (0, 0))
    spec = pl.BlockSpec((784, width), lambda i: (i, 0))
    return pl.pallas_call(
        input_kernel,
        grid=(rows // 784,),
        in_specs=[deltas, deltas, weights, weights, spec],
        out_specs=spec,
        out_shape=jax.ShapeDtypeStruct((rows, width), bf16),
        compiler_params=params(),
        cost_estimate=cost(4 * rows * width * half, 0),
    )(delta_own, delta_other, own, other, tokens)


def hidden_kernel(core_ref, normed_ref, own_ref, other_ref, hidden_ref):
    normed = normed_ref[...]
    half, step = own_ref.shape[1], 256
    for which, weights_ref in ((0, own_ref), (1, other_ref)):
        start = jnp.where(core_ref[0] == which, 0, half)
        for n in range(0, half, step):
            pre = jnp.dot(normed, weights_ref[:, n : n + step], preferred_element_type=f32)
            columns = pl.ds(pl.multiple_of(start + n, step), step)
            hidden_ref[:, columns] = gelu_parts(pre)[0].astype(bf16)


def hidden_call(normed, own, other, core):
    rows, width = normed.shape
    half, tile = own.shape[1], rows // 2
    weights = pl.BlockSpec((width, half), lambda i, core: (0, 0))
    return pl.pallas_call(
        hidden_kernel,
        grid_spec=pltpu.PrefetchScalarGridSpec(
            num_scalar_prefetch=1,
            grid=(rows // tile,),
            in_specs=[pl.BlockSpec((tile, width), lambda i, core: (i, 0)), weights, weights],
            out_specs=pl.BlockSpec((tile, 2 * half), lambda i, core: (i, 0)),
        ),
        out_shape=jax.ShapeDtypeStruct((rows, 2 * half), bf16),
        compiler_params=params(),
        cost_estimate=cost(4 * rows * width * half, 0),
    )(core.astype(jnp.int32).reshape(1), normed, own, other)


def step_reduce(kept, got):
    kept = kept.reshape(2, 2, 2, 2, 64, -1)
    got = got.reshape(kept.shape)
    total = None
    for step in ((0, 0),) + STEPS:
        zl, xl = class_of(step)
        start, size = (0, zl, 0, xl, 0, 0), (2, 1, 2, 1) + kept.shape[4:]
        piece = lax.dynamic_slice(kept, start, size) + lax.dynamic_slice(got, start, size).astype(f32)
        if step == (0, 0):
            total = piece
        else:
            total = total + shifted(piece.astype(bf16), step, -1).astype(f32)
    return total.astype(bf16).reshape((4,) + kept.shape[4:])


def per_device(tokens, cotangent, global_tokens, master, first_moment, second_moment, teacher):
    core = lax.axis_index("core")
    yh = lax.axis_index("yh")

    rounded = jnp.stack([master.astype(bf16), teacher.astype(bf16)])
    pair = in_order(columns_of(rounded, core), swap(columns_of(rounded, 1 - core)), "core", 1)
    blocks = in_order(pair, across(pair), "yh", 1)
    blocks, tokens, global_tokens = lax.optimization_barrier((blocks, tokens, global_tokens))
    both_parts = even_gather(blocks)
    normed, teacher_normed, both_parts = lax.optimization_barrier(
        (norm_call(tokens), norm_call(global_tokens), both_parts)
    )
    weights_own = assemble(steps_of(both_parts[:, 0]))
    normed, weights_own, teacher_part = lax.optimization_barrier(
        (normed, weights_own, both_parts[:, 1])
    )
    weights_other = swap(weights_own)

    def delta_of(weights, which):
        preact = jnp.dot(normed, weights, preferred_element_type=f32)
        unused, slope = gelu_parts(preact)
        return (columns_of(cotangent, which).astype(f32) * slope).astype(bf16)

    def gradient_of(delta):
        return lax.dot_general(normed, delta, (((0,), (0,)), ((), ())), preferred_element_type=f32)

    delta_own = delta_of(weights_own, core)
    teacher_parts = steps_of(teacher_part)
    delta_own, weights_other = lax.optimization_barrier((delta_own, weights_other))
    delta_other = delta_of(weights_other, 1 - core)
    given, teacher_parts = lax.optimization_barrier(
        (gradient_of(delta_other).astype(bf16), teacher_parts)
    )
    kept, delta_own, delta_other = lax.optimization_barrier(
        (gradient_of(delta_own), delta_own, delta_other)
    )
    class_sum = step_reduce(kept, swap(given))
    grad_input = input_call(delta_own, delta_other, weights_own, weights_other, tokens)

    class_sum, grad_input, teacher_parts = lax.optimization_barrier(
        (class_sum, grad_input, teacher_parts)
    )
    pieces = lax.all_to_all(class_sum, EVEN, 0, 0, tiled=True)
    teacher_own = assemble(teacher_parts)
    teacher_hidden = hidden_call(teacher_normed, teacher_own, swap(teacher_own), core)

    pieces, teacher_hidden = lax.optimization_barrier((pieces, teacher_hidden))

    plane = jnp.sum(pieces.astype(f32), axis=0)
    mine = lax.dynamic_slice_in_dim(plane, yh * 32, 32, axis=0)
    other = lax.dynamic_slice_in_dim(plane, (1 - yh) * 32, 32, axis=0)
    group = mine + across(other.astype(bf16)).astype(f32)
    group = lax.optimization_barrier(group.astype(bf16))
    group = group.astype(f32) + lax.ppermute(group, "yl", SWAP).astype(f32)
    mine = lax.dynamic_slice_in_dim(group, core * 16, 16, axis=0)
    other = lax.dynamic_slice_in_dim(group, (1 - core) * 16, 16, axis=0)
    gradient = in_order(mine, swap(other), "core", 1)
    new_master, new_first, new_second, new_teacher = adamw_update(
        gradient, master, first_moment, second_moment, teacher
    )
    return (grad_input, teacher_hidden, new_master, new_first, new_second, new_teacher)


def solution(mesh):
    names = ("zh", "zl", "xh", "xl", "yh", "core", "yl")
    split = Mesh(mesh.devices.reshape((2,) * 7), names)
    tokens = P(names, None)
    rows = P(names[:-1], None)
    return jax.shard_map(
        per_device,
        mesh=split,
        in_specs=(tokens, tokens, tokens, rows, rows, rows, rows),
        out_specs=(tokens, tokens, rows, rows, rows, rows),
        check_vma=False,
    )
```

time: 210 us -> 140 us (0.67)
  blocking collectives: 74.5 us -> 0 us
  starting transfers between devices: 6.83 us -> 42.4 us
  waiting for transfers between devices: 57.4 us -> 28 us
  Pallas kernels: 0 us -> 27.4 us
  matrix products: 42.7 us -> 25.6 us
  between operations: 14.2 us -> 0.97 us
  local copies, waits for them, and re-layouts: 0.33 us -> 8.49 us
  other arithmetic: 14 us -> 6.74 us
    all_to_all x2 -> x0, blocking collectives: 74.5 us -> none  [the longest x1 40.4 us: per_device(): weights_own = lax.all_to_all(copies, CHIPS, 0, 0, tiled=True)]
    all_gather x1 -> x0, waiting for transfers between devices: 50.5 us -> none  [per_device(): lax.all_gather(teacher.astype(bf16), ('z', 'x', 'yh', 'core'), axis=0, ti...]
    pallas_call x0 -> x6, Pallas kernels: none -> 27.4 us  [the longest x1 12.6 us: input_call(): pl.pallas_call(input_kernel, grid=(rows // 784,), in_specs=[deltas, delta...]
    ppermute x0 -> x11, starting transfers between devices: none -> 21.5 us  [the longest x9 16 us: shifted(): return lax.ppermute(block, ('zh', 'zl', 'xh', 'xl'), moves)]
    dot_general x3 -> x0, matrix products: 18.6 us -> none  [the longest x1 8.03 us: per_device(): jnp.dot(teacher_centred.astype(bf16), teacher_weights, preferred_element_...]
    ppermute x0 -> x11, waiting for transfers between devices: none -> 14 us  [the longest x9 8.73 us: shifted(): return lax.ppermute(block, ('zh', 'zl', 'xh', 'xl'), moves)]
    all_to_all x0 -> x2, starting transfers between devices: none -> 10.9 us  [the longest x1 7.23 us: even_gather(): return lax.all_to_all(copies, EVEN, 0, 0, tiled=True)]
    all_to_all x0 -> x2, waiting for transfers between devices: none -> 8.9 us  [the longest x1 8.27 us: even_gather(): return lax.all_to_all(copies, EVEN, 0, 0, tiled=True)]
  transfers between devices with their start and end apart: 6 -> 19, of which waited for: 5 -> 11; matrix products, arithmetic and copies ran while one was open for 13% -> 18% of each run, Pallas kernels for 0% -> 17%
where the time goes in v2:
time: 140 us
  starting transfers between devices  42.4 us (30%)
  waiting for transfers between devices  28 us (20%)
  Pallas kernels  27.4 us (20%)
  matrix products  25.6 us (18%)
  local copies, waits for them, and re-layouts  8.49 us (6%)
  other arithmetic  6.74 us (5%)
    ppermute x9, starting transfers between devices, shifted(): return lax.ppermute(block, ('zh', 'zl', 'xh', 'xl'), moves)  16 us
    dot_general x2, matrix products, delta_of(): preact = jnp.dot(normed, weights, preferred_element_type=f32)  14.2 us
    pallas_call x1, Pallas kernels, input_call(): pl.pallas_call(input_kernel, grid=(rows // 784,), in_specs=[deltas, delta...  12.6 us
    dot_general x2, matrix products, gradient_of(): lax.dot_general(normed, delta, (((0,), (0,)), ((), ())), preferred_elemen...  11.3 us
    ppermute x5, starting transfers between devices, swap(): return lax.ppermute(block, 'core', SWAP)  9.9 us
    ppermute x9, waiting for transfers between devices, shifted(): return lax.ppermute(block, ('zh', 'zl', 'xh', 'xl'), moves)  8.73 us
    all_to_all x1, waiting for transfers between devices, even_gather(): return lax.all_to_all(copies, EVEN, 0, 0, tiled=True)  8.27 us
    all_to_all x1, starting transfers between devices, even_gather(): return lax.all_to_all(copies, EVEN, 0, 0, tiled=True)  7.23 us
  transfers between devices with their start and end apart: 19, of which 11 were waited for; matrix products, arithmetic and copies ran while one was open for 18% of the time, Pallas kernels for 17%

profile of v2, /device:TPU:1, one launch (start us, length us, event | category | flops | bytes accessed | tf_op | source)
XLA Modules:
  0.0 139.5 jit_solution(13778675542919528619)
XLA Ops:
  4.1 2.9 %collective-permute-start.1 = (bf16[2,32,1024]{2,1,0:T(8,128)(2,1)S(1)}, bf16[2,32,1024]{2,1,0:T(8,128)(2,1)S(1)}, u32[]{:S(2)}, u32[]{:S(2)}) collective-permute-start(bf16[2,32,1024]{2,1,0:T(8,128)(2,1)S(1)} %maximum_select_fusion.1), channel_id=1, source_target_pairs={{0,5},{5,0},{1,4},{4,1},{2,7},{7,2},{3,6},{6,3},{8,13},{13,8},{9,1... | collective-permute-start | bytes 393224 | tf_op jit(solution)/shard_map/ppermute | solution.py:64
  7.0 3.4 %collective-permute-done.1 = bf16[2,32,1024]{2,1,0:T(8,128)(2,1)S(1)} collective-permute-done((bf16[2,32,1024]{2,1,0:T(8,128)(2,1)S(1)}, bf16[2,32,1024]{2,1,0:T(8,128)(2,1)S(1)}, u32[]{:S(2)}, u32[]{:S(2)}) %collective-permute-start.1) | collective-permute-done | bytes 131104 | tf_op jit(solution)/shard_map/ppermute | solution.py:64
  11.6 7.2 %all-to-all-start = ((bf16[4,2,64,1024]{3,2,1,0:T(8,128)(2,1)}), bf16[4,2,64,1024]{3,2,1,0:T(8,128)(2,1)}, u32[]{:S(2)}, u32[]{:S(2)}) async-start(bf16[4,2,64,1024]{3,2,1,0:T(8,128)(2,1)} %broadcast_in_dim.2), calls=%async_computation | async-start | bytes 2097152 | tf_op jit(solution)/shard_map/all_to_all | solution.py:92
  18.8 3.5 %shard_map.118 = bf16[1568,1024]{1,0:T(8,128)(2,1)S(1)} custom-call(bf16[1568,1024]{1,0:T(8,128)(2,1)} %tokens_ref.2), custom_call_target="tpu_custom_call" | custom-call | bytes 1024 | tf_op jit(solution)/shard_map/pallas_call | solution.py:142
  24.4 8.3 %all-to-all-done = bf16[4,2,64,1024]{3,2,1,0:T(8,128)(2,1)} async-done(((bf16[4,2,64,1024]{3,2,1,0:T(8,128)(2,1)}), bf16[4,2,64,1024]{3,2,1,0:T(8,128)(2,1)}, u32[]{:S(2)}, u32[]{:S(2)}) %all-to-all-start) | async-done | bytes 1048608 | tf_op jit(solution)/shard_map/all_to_all | solution.py:92
  32.7 2.2 %slice_bitcast_fusion = (bf16[4,64,1024]{2,1,0:T(8,128)(2,1)}, bf16[4,64,1024]{2,1,0:T(8,128)(2,1)}) fusion(bf16[4,2,64,1024]{3,2,1,0:T(8,128)(2,1)} %all-to-all-done), kind=kLoop, calls=%fused_computation.20 | loop fusion | bytes 2097152 | tf_op jit(solution)/shard_map/squeeze | solution.py:238
  35.9 4.2 %collective-permute-start.4 = (bf16[4,64,1024]{2,1,0:T(8,128)(2,1)}, bf16[4,64,1024]{2,1,0:T(8,128)(2,1)}, u32[]{:S(2)}, u32[]{:S(2)}) collective-permute-start(bf16[4,64,1024]{2,1,0:T(8,128)(2,1)} %get-tuple-element.68.refs_0_), channel_id=1, source_target_pairs={{0,120},{8,96},{16,104},{24,112},{32,24},{40,0},{48,8},{56,16},{64... | collective-permute-start | bytes 1572872 | tf_op jit(solution)/shard_map/ppermute | solution.py:73
  40.2 7.6 %collective-permute-done.2.refs_1_ = bf16[4,64,1024]{2,1,0:T(8,128)(2,1)} collective-permute-done((bf16[4,64,1024]{2,1,0:T(8,128)(2,1)}, bf16[4,64,1024]{2,1,0:T(8,128)(2,1)}, u32[]{:S(2)}, u32[]{:S(2)}) %collective-permute-start.2) | collective-permute-done | bytes 524320 | tf_op jit(solution)/shard_map/ppermute | solution.py:73
  48.9 2.2 %shard_map.120.own_ref = bf16[1024,1024]{1,0:T(8,128)(2,1)S(1)} custom-call(s32[2]{0:T(128)S(1)} %pad_add_fusion.class_ref, bf16[4,64,1024]{2,1,0:T(8,128)(2,1)} %get-tuple-element.68.refs_0_, bf16[4,64,1024]{2,1,0:T(8,128)(2,1)} %collective-permute-done.2.refs_1_, bf16[4,64,1024]{2,1,0:T(8,128)(2,1)} %collective-permute-done.3.refs_2_, ...), custom_call_target="tpu_custom_call" | custom-call | bytes 4194304 | tf_op jit(solution)/shard_map/pallas_call | solution.py:117
  51.2 3.7 %collective-permute-start.5 = (bf16[1024,1024]{1,0:T(8,128)(2,1)S(1)}, bf16[1024,1024]{1,0:T(8,128)(2,1)S(1)}, u32[]{:S(2)}, u32[]{:S(2)}) collective-permute-start(bf16[1024,1024]{1,0:T(8,128)(2,1)S(1)} %shard_map.120.own_ref), channel_id=1, source_target_pairs={{0,2},{2,0},{1,3},{3,1},{4,6},{6,4},{5,7},{7,5},{8,10},{10,8},{9,1... | collective-permute-start | bytes 6291464 | tf_op jit(solution)/shard_map/ppermute | solution.py:60
  55.9 4.6 %collective-permute-start.8 = (bf16[4,64,1024]{2,1,0:T(8,128)(2,1)S(1)}, bf16[4,64,1024]{2,1,0:T(8,128)(2,1)S(1)}, u32[]{:S(2)}, u32[]{:S(2)}) collective-permute-start(bf16[4,64,1024]{2,1,0:T(8,128)(2,1)S(1)} %copy-done.2), channel_id=1, source_target_pairs={{0,120},{8,96},{16,104},{24,112},{32,24},{40,0},{48,8},{56,16},{64... | collective-permute-start | bytes 1572872 | tf_op jit(solution)/shard_map/ppermute | solution.py:73
  60.6 8.3 %fusion.5.delta_own_ref = bf16[1568,1024]{1,0:T(8,128)(2,1)} fusion(bf16[1568,2048]{1,0:T(8,128)(2,1)} %param.8, s32[]{:T(128)S(6)} %select_n.105, bf16[1568,1024]{1,0:T(8,128)(2,1)S(1)} %shard_map.118, bf16[1024,1024]{1,0:T(8,128)(2,1)S(1)} %shard_map.120.own_ref), kind=kOutput, calls=%fused_computation.7 | convolution fusion | flops 3305996288 | bytes 11730948 | tf_op jit(solution)/shard_map/dot_general | solution.py:243
  68.9 6.0 %fusion.11.delta_other_ref = bf16[1568,1024]{1,0:T(8,128)(2,1)S(1)} fusion(bf16[1568,2048]{1,0:T(8,128)(2,1)S(1)} %bitcast.25, s32[]{:T(128)S(6)} %select_n.106, bf16[1568,1024]{1,0:T(8,128)(2,1)S(1)} %shard_map.118, bf16[1024,1024]{1,0:T(8,128)(2,1)S(1)} %collective-permute-done.5.other_ref), kind=kOutput, calls=%fused_computation.13 | convolution fusion | flops 3305996288 | bytes 11730948 | tf_op jit(solution)/shard_map/dot_general | solution.py:243
  74.8 5.3 %convolution_convert_fusion = bf16[1024,1024]{1,0:T(8,128)(2,1)} fusion(bf16[1568,1024]{1,0:T(8,128)(2,1)S(1)} %shard_map.118, bf16[1568,1024]{1,0:T(8,128)(2,1)S(1)} %fusion.11.delta_other_ref), kind=kOutput, calls=%fused_computation.14 | convolution fusion | flops 3289382912 | bytes 8519680 | tf_op jit(solution)/shard_map/dot_general | solution.py:248
  83.1 6.1 %fusion.16 = f32[1024,1024]{1,0:T(8,128)S(1)} fusion(bf16[1568,1024]{1,0:T(8,128)(2,1)S(1)} %shard_map.118, bf16[1568,1024]{1,0:T(8,128)(2,1)} %fusion.5.delta_own_ref), kind=kOutput, calls=%fused_computation.44 | convolution fusion | flops 3288334336 | bytes 10616832 | tf_op jit(solution)/shard_map/dot_general | solution.py:248
  91.4 2.3 %collective-permute-start.11 = (bf16[2,1,2,1,64,1024]{5,4,3,2,1,0:T(8,128)(2,1)S(1)}, bf16[2,1,2,1,64,1024]{5,4,3,2,1,0:T(8,128)(2,1)S(1)}, u32[]{:S(2)}, u32[]{:S(2)}) collective-permute-start(bf16[2,1,2,1,64,1024]{5,4,3,2,1,0:T(8,128)(2,1)S(1)} %get-tuple-element.66), channel_id=1, source_target_pairs={{0,24},{8,0},{16,8},{24,16},{32,56},{40,32},{48,40},{56,48},{64,88... | collective-permute-start | bytes 1572872 | tf_op jit(solution)/shard_map/ppermute | solution.py:73
  93.7 2.8 %collective-permute-start.10 = (bf16[2,1,2,1,64,1024]{5,4,3,2,1,0:T(8,128)(2,1)S(1)}, bf16[2,1,2,1,64,1024]{5,4,3,2,1,0:T(8,128)(2,1)S(1)}, u32[]{:S(2)}, u32[]{:S(2)}) collective-permute-start(bf16[2,1,2,1,64,1024]{5,4,3,2,1,0:T(8,128)(2,1)S(1)} %get-tuple-element.64), channel_id=1, source_target_pairs={{0,96},{8,104},{16,112},{24,120},{32,0},{40,8},{48,16},{56,24},{64... | collective-permute-start | bytes 1572872 | tf_op jit(solution)/shard_map/ppermute | solution.py:73
  96.5 12.6 %shard_map.121 = bf16[1568,1024]{1,0:T(8,128)(2,1)} custom-call(bf16[1568,1024]{1,0:T(8,128)(2,1)} %fusion.5.delta_own_ref, bf16[1568,1024]{1,0:T(8,128)(2,1)} %copy-done.19, bf16[1024,1024]{1,0:T(8,128)(2,1)S(1)} %copy-done.1, bf16[1024,1024]{1,0:T(8,128)(2,1)S(1)} %copy-done.14, bf16[1568,1024]{1,0:T(8,128)(2,1)} %tokens_ref.2), custom_call_target="tpu_custom_call" | custom-call | flops 6576668672 | tf_op jit(solution)/shard_map/pallas_call | solution.py:169
  109.2 2.4 %add_convert_fusion = bf16[2,1,2,1,64,1024]{5,4,3,2,1,0:T(8,128)(2,1)} fusion(bf16[2,1,2,1,64,1024]{5,4,3,2,1,0:T(8,128)(2,1)S(1)} %collective-permute-done.12, bf16[2,1,2,1,64,1024]{5,4,3,2,1,0:T(8,128)(2,1)S(1)} %collective-permute-done.11, bf16[2,1,2,1,64,1024]{5,4,3,2,1,0:T(8,128)(2,1)S(1)} %collective-permute-done.10, ...), kind=kLoop, calls=%fused_computation.16 | loop fusion | flops 2359296 | bytes 3670024 | tf_op jit(solution)/shard_map/convert_element_type | solution.py:221
  113.7 3.7 %all-to-all-start.1 = ((bf16[4,64,1024]{2,1,0:T(8,128)(2,1)}), bf16[4,64,1024]{2,1,0:T(8,128)(2,1)S(1)}, u32[]{:S(2)}, u32[]{:S(2)}) async-start(bf16[4,64,1024]{2,1,0:T(8,128)(2,1)} %bitcast.8), calls=%async_computation.1 | async-start | bytes 1048576 | tf_op jit(solution)/shard_map/all_to_all | solution.py:266
  119.0 7.1 %shard_map.123 = bf16[784,2048]{1,0:T(8,128)(2,1)} custom-call(s32[1]{0:T(128)} %bitcast.9.core_ref, bf16[784,1024]{1,0:T(8,128)(2,1)S(1)} %copy-done.6, bf16[1024,1024]{1,0:T(8,128)(2,1)S(1)} %shard_map.122.own_ref, bf16[1024,1024]{1,0:T(8,128)(2,1)} %collective-permute-done.13.other_ref), custom_call_target="tpu_custom_call" | custom-call | flops 3288334336 | tf_op jit(solution)/shard_map/pallas_call | solution.py:195
  126.9 2.6 %collective-permute-start.14 = (bf16[32,1024]{1,0:T(8,128)(2,1)S(1)}, bf16[32,1024]{1,0:T(8,128)(2,1)S(1)}, u32[]{:S(2)}, u32[]{:S(2)}) collective-permute-start(bf16[32,1024]{1,0:T(8,128)(2,1)S(1)} %dynamic-slice_convert_fusion), channel_id=1, source_target_pairs={{0,5},{5,0},{1,4},{4,1},{2,7},{7,2},{3,6},{6,3},{8,13},{13,8},{9,1... | collective-permute-start | bytes 196616 | tf_op jit(solution)/shard_map/ppermute | solution.py:64
  131.4 3.1 %collective-permute-done.15 = bf16[32,1024]{1,0:T(8,128)(2,1)S(1)} collective-permute-done((bf16[32,1024]{1,0:T(8,128)(2,1)S(1)}, bf16[32,1024]{1,0:T(8,128)(2,1)S(1)}, u32[]{:S(2)}, u32[]{:S(2)}) %collective-permute-start.15) | collective-permute-done | bytes 65568 | tf_op jit(solution)/shard_map/ppermute | solution.py:277
  134.5 3.2 %collective-permute-start.16 = (f32[16,1024]{1,0:T(8,128)S(1)}, f32[16,1024]{1,0:T(8,128)S(1)}, u32[]{:S(2)}, u32[]{:S(2)}) collective-permute-start(f32[16,1024]{1,0:T(8,128)S(1)} %get-tuple-element.69), channel_id=1, source_target_pairs={{0,2},{2,0},{1,3},{3,1},{4,6},{6,4},{5,7},{7,5},{8,10},{10,8},{9,1... | collective-permute-start | bytes 196616 | tf_op jit(solution)/shard_map/ppermute | solution.py:60
  (84 shorter events, 23.3 us)
Async XLA Ops:
  1.7 2.4 %collective-permute-start = (bf16[2,16,1024]{2,1,0:T(8,128)(2,1)S(1)}, bf16[2,16,1024]{2,1,0:T(8,128)(2,1)S(1)}, u32[]{:S(2)}, u32[]{:S(2)}) collective-permute-start(bf16[2,16,1024]{2,1,0:T(8,128)(2,1)S(1)} %get-tuple-element.72), channel_id=1, source_target_pairs={{0,2},{2,0},{1,3},{3,1},{4,6},{6,4},{5,7},{7,5},{8,10},{10,8},{9,1... | collective-permute-start | bytes 196616 | tf_op jit(solution)/shard_map/ppermute | solution.py:60
  4.1 6.3 %collective-permute-start.1 = (bf16[2,32,1024]{2,1,0:T(8,128)(2,1)S(1)}, bf16[2,32,1024]{2,1,0:T(8,128)(2,1)S(1)}, u32[]{:S(2)}, u32[]{:S(2)}) collective-permute-start(bf16[2,32,1024]{2,1,0:T(8,128)(2,1)S(1)} %maximum_select_fusion.1), channel_id=1, source_target_pairs={{0,5},{5,0},{1,4},{4,1},{2,7},{7,2},{3,6},{6,3},{8,13},{13,8},{9,1... | collective-permute-start | bytes 393224 | tf_op jit(solution)/shard_map/ppermute | solution.py:64
  11.6 21.1 %all-to-all-start = ((bf16[4,2,64,1024]{3,2,1,0:T(8,128)(2,1)}), bf16[4,2,64,1024]{3,2,1,0:T(8,128)(2,1)}, u32[]{:S(2)}, u32[]{:S(2)}) async-start(bf16[4,2,64,1024]{3,2,1,0:T(8,128)(2,1)} %broadcast_in_dim.2), calls=%async_computation | async-start | bytes 2097152 | tf_op jit(solution)/shard_map/all_to_all | solution.py:92
  34.9 12.9 %collective-permute-start.2 = (bf16[4,64,1024]{2,1,0:T(8,128)(2,1)}, bf16[4,64,1024]{2,1,0:T(8,128)(2,1)}, u32[]{:S(2)}, u32[]{:S(2)}) collective-permute-start(bf16[4,64,1024]{2,1,0:T(8,128)(2,1)} %get-tuple-element.68.refs_0_), channel_id=1, source_target_pairs={{0,32},{8,40},{16,48},{24,56},{32,64},{40,72},{48,80},{56,88},{64,... | collective-permute-start | bytes 1572872 | tf_op jit(solution)/shard_map/ppermute | solution.py:73
  35.6 12.3 %collective-permute-start.3 = (bf16[4,64,1024]{2,1,0:T(8,128)(2,1)}, bf16[4,64,1024]{2,1,0:T(8,128)(2,1)}, u32[]{:S(2)}, u32[]{:S(2)}) collective-permute-start(bf16[4,64,1024]{2,1,0:T(8,128)(2,1)} %get-tuple-element.68.refs_0_), channel_id=1, source_target_pairs={{0,8},{8,16},{16,24},{24,0},{32,40},{40,48},{48,56},{56,32},{64,72... | collective-permute-start | bytes 1572872 | tf_op jit(solution)/shard_map/ppermute | solution.py:73
  35.9 13.0 %collective-permute-start.4 = (bf16[4,64,1024]{2,1,0:T(8,128)(2,1)}, bf16[4,64,1024]{2,1,0:T(8,128)(2,1)}, u32[]{:S(2)}, u32[]{:S(2)}) collective-permute-start(bf16[4,64,1024]{2,1,0:T(8,128)(2,1)} %get-tuple-element.68.refs_0_), channel_id=1, source_target_pairs={{0,120},{8,96},{16,104},{24,112},{32,24},{40,0},{48,8},{56,16},{64... | collective-permute-start | bytes 1572872 | tf_op jit(solution)/shard_map/ppermute | solution.py:73
  51.2 17.6 %copy-start = (bf16[1024,1024]{1,0:T(8,128)(2,1)}, bf16[1024,1024]{1,0:T(8,128)(2,1)S(1)}, u32[]{:S(2)}) copy-start(bf16[1024,1024]{1,0:T(8,128)(2,1)S(1)} %shard_map.120.own_ref) | copy-start | bytes 6291460
  51.2 17.6 %collective-permute-start.5 = (bf16[1024,1024]{1,0:T(8,128)(2,1)S(1)}, bf16[1024,1024]{1,0:T(8,128)(2,1)S(1)}, u32[]{:S(2)}, u32[]{:S(2)}) collective-permute-start(bf16[1024,1024]{1,0:T(8,128)(2,1)S(1)} %shard_map.120.own_ref), channel_id=1, source_target_pairs={{0,2},{2,0},{1,3},{3,1},{4,6},{6,4},{5,7},{7,5},{8,10},{10,8},{9,1... | collective-permute-start | bytes 6291464 | tf_op jit(solution)/shard_map/ppermute | solution.py:60
  55.0 25.2 %collective-permute-start.6 = (bf16[4,64,1024]{2,1,0:T(8,128)(2,1)S(1)}, bf16[4,64,1024]{2,1,0:T(8,128)(2,1)S(1)}, u32[]{:S(2)}, u32[]{:S(2)}) collective-permute-start(bf16[4,64,1024]{2,1,0:T(8,128)(2,1)S(1)} %copy-done.2), channel_id=1, source_target_pairs={{0,32},{8,40},{16,48},{24,56},{32,64},{40,72},{48,80},{56,88},{64,... | collective-permute-start | bytes 1572872 | tf_op jit(solution)/shard_map/ppermute | solution.py:73
  55.5 25.4 %collective-permute-start.7 = (bf16[4,64,1024]{2,1,0:T(8,128)(2,1)S(1)}, bf16[4,64,1024]{2,1,0:T(8,128)(2,1)S(1)}, u32[]{:S(2)}, u32[]{:S(2)}) collective-permute-start(bf16[4,64,1024]{2,1,0:T(8,128)(2,1)S(1)} %copy-done.2), channel_id=1, source_target_pairs={{0,8},{8,16},{16,24},{24,0},{32,40},{40,48},{48,56},{56,32},{64,72... | collective-permute-start | bytes 1572872 | tf_op jit(solution)/shard_map/ppermute | solution.py:73
  55.9 25.9 %collective-permute-start.8 = (bf16[4,64,1024]{2,1,0:T(8,128)(2,1)S(1)}, bf16[4,64,1024]{2,1,0:T(8,128)(2,1)S(1)}, u32[]{:S(2)}, u32[]{:S(2)}) collective-permute-start(bf16[4,64,1024]{2,1,0:T(8,128)(2,1)S(1)} %copy-done.2), channel_id=1, source_target_pairs={{0,120},{8,96},{16,104},{24,112},{32,24},{40,0},{48,8},{56,16},{64... | collective-permute-start | bytes 1572872 | tf_op jit(solution)/shard_map/ppermute | solution.py:73
  82.6 6.6 %collective-permute-start.9 = (bf16[1024,1024]{1,0:T(8,128)(2,1)}, bf16[1024,1024]{1,0:T(8,128)(2,1)}, u32[]{:S(2)}, u32[]{:S(2)}) collective-permute-start(bf16[1024,1024]{1,0:T(8,128)(2,1)} %convolution_convert_fusion), channel_id=1, source_target_pairs={{0,2},{2,0},{1,3},{3,1},{4,6},{6,4},{5,7},{7,5},{8,10},{10,8},{9,1... | collective-permute-start | bytes 6291464 | tf_op jit(solution)/shard_map/ppermute | solution.py:60
  91.4 17.8 %collective-permute-start.12 = (bf16[2,1,2,1,64,1024]{5,4,3,2,1,0:T(8,128)(2,1)S(1)}, bf16[2,1,2,1,64,1024]{5,4,3,2,1,0:T(8,128)(2,1)S(1)}, u32[]{:S(2)}, u32[]{:S(2)}) collective-permute-start(bf16[2,1,2,1,64,1024]{5,4,3,2,1,0:T(8,128)(2,1)S(1)} %get-tuple-element.65), channel_id=1, source_target_pairs={{0,40},{8,48},{16,56},{24,32},{32,72},{40,80},{48,88},{56,64},{64,... | collective-permute-start | bytes 1572872 | tf_op jit(solution)/shard_map/ppermute | solution.py:73
  91.4 17.7 %collective-permute-start.11 = (bf16[2,1,2,1,64,1024]{5,4,3,2,1,0:T(8,128)(2,1)S(1)}, bf16[2,1,2,1,64,1024]{5,4,3,2,1,0:T(8,128)(2,1)S(1)}, u32[]{:S(2)}, u32[]{:S(2)}) collective-permute-start(bf16[2,1,2,1,64,1024]{5,4,3,2,1,0:T(8,128)(2,1)S(1)} %get-tuple-element.66), channel_id=1, source_target_pairs={{0,24},{8,0},{16,8},{24,16},{32,56},{40,32},{48,40},{56,48},{64,88... | collective-permute-start | bytes 1572872 | tf_op jit(solution)/shard_map/ppermute | solution.py:73
  93.7 15.4 %collective-permute-start.10 = (bf16[2,1,2,1,64,1024]{5,4,3,2,1,0:T(8,128)(2,1)S(1)}, bf16[2,1,2,1,64,1024]{5,4,3,2,1,0:T(8,128)(2,1)S(1)}, u32[]{:S(2)}, u32[]{:S(2)}) collective-permute-start(bf16[2,1,2,1,64,1024]{5,4,3,2,1,0:T(8,128)(2,1)S(1)} %get-tuple-element.64), channel_id=1, source_target_pairs={{0,96},{8,104},{16,112},{24,120},{32,0},{40,8},{48,16},{56,24},{64... | collective-permute-start | bytes 1572872 | tf_op jit(solution)/shard_map/ppermute | solution.py:73
  112.7 4.9 %collective-permute-start.13 = (bf16[1024,1024]{1,0:T(8,128)(2,1)S(1)}, bf16[1024,1024]{1,0:T(8,128)(2,1)}, u32[]{:S(2)}, u32[]{:S(2)}) collective-permute-start(bf16[1024,1024]{1,0:T(8,128)(2,1)S(1)} %shard_map.122.own_ref), channel_id=1, source_target_pairs={{0,2},{2,0},{1,3},{3,1},{4,6},{6,4},{5,7},{7,5},{8,10},{10,8},{9,1... | collective-permute-start | bytes 6291464 | tf_op jit(solution)/shard_map/ppermute | solution.py:60
  113.7 13.1 %all-to-all-start.1 = ((bf16[4,64,1024]{2,1,0:T(8,128)(2,1)}), bf16[4,64,1024]{2,1,0:T(8,128)(2,1)S(1)}, u32[]{:S(2)}, u32[]{:S(2)}) async-start(bf16[4,64,1024]{2,1,0:T(8,128)(2,1)} %bitcast.8), calls=%async_computation.1 | async-start | bytes 1048576 | tf_op jit(solution)/shard_map/all_to_all | solution.py:266
  119.0 19.6 %copy-start.15 = (f32[16,2048]{1,0:T(8,128)S(1)}, f32[16,2048]{1,0:T(8,128)}, u32[]{:S(2)}) copy-start(f32[16,2048]{1,0:T(8,128)} %param.13) | copy-start | bytes 393220
  119.0 19.6 %copy-start.16 = (f32[16,2048]{1,0:T(8,128)S(1)}, f32[16,2048]{1,0:T(8,128)}, u32[]{:S(2)}) copy-start(f32[16,2048]{1,0:T(8,128)} %param.10) | copy-start | bytes 393220
  119.0 19.6 %copy-start.17 = (f32[16,2048]{1,0:T(8,128)S(1)}, f32[16,2048]{1,0:T(8,128)}, u32[]{:S(2)}) copy-start(f32[16,2048]{1,0:T(8,128)} %param.11) | copy-start | bytes 393220
  119.0 19.6 %copy-start.18 = (f32[16,2048]{1,0:T(8,128)S(1)}, f32[16,2048]{1,0:T(8,128)}, u32[]{:S(2)}) copy-start(f32[16,2048]{1,0:T(8,128)} %param.12) | copy-start | bytes 393220
  126.9 4.4 %collective-permute-start.14 = (bf16[32,1024]{1,0:T(8,128)(2,1)S(1)}, bf16[32,1024]{1,0:T(8,128)(2,1)S(1)}, u32[]{:S(2)}, u32[]{:S(2)}) collective-permute-start(bf16[32,1024]{1,0:T(8,128)(2,1)S(1)} %dynamic-slice_convert_fusion), channel_id=1, source_target_pairs={{0,5},{5,0},{1,4},{4,1},{2,7},{7,2},{3,6},{6,3},{8,13},{13,8},{9,1... | collective-permute-start | bytes 196616 | tf_op jit(solution)/shard_map/ppermute | solution.py:64
  131.3 3.2 %collective-permute-start.15 = (bf16[32,1024]{1,0:T(8,128)(2,1)S(1)}, bf16[32,1024]{1,0:T(8,128)(2,1)S(1)}, u32[]{:S(2)}, u32[]{:S(2)}) collective-permute-start(bf16[32,1024]{1,0:T(8,128)(2,1)S(1)} %add_convert_fusion.4), channel_id=1, source_target_pairs={{0,1},{1,0},{2,3},{3,2},{4,5},{5,4},{6,7},{7,6},{8,9},{9,8},{10,11... | collective-permute-start | bytes 196616 | tf_op jit(solution)/shard_map/ppermute | solution.py:277
  134.5 4.1 %collective-permute-start.16 = (f32[16,1024]{1,0:T(8,128)S(1)}, f32[16,1024]{1,0:T(8,128)S(1)}, u32[]{:S(2)}, u32[]{:S(2)}) collective-permute-start(f32[16,1024]{1,0:T(8,128)S(1)} %get-tuple-element.69), channel_id=1, source_target_pairs={{0,2},{2,0},{1,3},{3,1},{4,6},{6,4},{5,7},{7,5},{8,10},{10,8},{9,1... | collective-permute-start | bytes 196616 | tf_op jit(solution)/shard_map/ppermute | solution.py:60
  (17 other events, 94.6 us)

commit v3 on v1

v3 whole, which is shorter than its diff:
```python
import math

import jax
import jax.numpy as jnp
from jax import lax
from jax.experimental import pallas as pl
from jax.experimental.pallas import tpu as pltpu
from jax.sharding import Mesh
from jax.sharding import PartitionSpec as P

beta_one = 0.9
beta_two = 0.999
learn_rate = 0.001
decay_rate = 0.04
ema_momentum = 0.996
adam_epsilon = 1e-08
norm_epsilon = 1e-06
bias_one = 0.9999734386011124
bias_two = 0.09520785288629038

SWAP = [(0, 1), (1, 0)]
CHIPS = ("z", "x", "yh")
bf16, f32 = jnp.bfloat16, jnp.float32


def params(mebibytes):
    return pltpu.CompilerParams(vmem_limit_bytes=mebibytes * 1024 * 1024)


def cost(flops, bytes_accessed):
    return pl.CostEstimate(flops=flops, bytes_accessed=bytes_accessed, transcendentals=0)


def layer_norm(block_tokens):
    values = block_tokens.astype(f32)
    middle = jnp.mean(values, axis=-1, keepdims=True)
    centred = values - middle
    inv_std = lax.rsqrt(jnp.mean(centred * centred, axis=-1, keepdims=True) + norm_epsilon)
    return (centred * inv_std, inv_std)


def gelu_parts(preact):
    cumul = 0.5 * (1.0 + lax.erf(preact * (1.0 / math.sqrt(2.0))))
    slope = cumul + preact * jnp.exp(-0.5 * preact * preact) * (1.0 / math.sqrt(2.0 * math.pi))
    return (preact * cumul, slope)


def adamw_update(gradient, master_rows, first_rows, second_rows, teacher_rows):
    new_first = beta_one * first_rows + (1.0 - beta_one) * gradient
    new_second = beta_two * second_rows + (1.0 - beta_two) * gradient * gradient
    update = new_first / bias_one / (jnp.sqrt(new_second / bias_two) + adam_epsilon)
    new_master = master_rows - learn_rate * (update + decay_rate * master_rows)
    new_teacher = ema_momentum * teacher_rows + (1.0 - ema_momentum) * new_master
    return (new_master, new_first, new_second, new_teacher)


def swap(block):
    return lax.ppermute(block, "core", SWAP)


def in_order(mine, theirs, axis_name, axis):
    first = lax.axis_index(axis_name) == 0
    return jnp.where(
        first,
        jnp.concatenate([mine, theirs], axis=axis),
        jnp.concatenate([theirs, mine], axis=axis),
    )


def columns_of(array, core):
    half = array.shape[-1] // 2
    return lax.dynamic_slice_in_dim(array, core * half, half, axis=array.ndim - 1)


def half_block(rows, core):
    return in_order(columns_of(rows, core), swap(columns_of(rows, 1 - core)), "core", 0)


def copies_of(block):
    return jnp.broadcast_to(block[None], (32,) + block.shape)


def exchanged(blocks):
    return lax.all_to_all(blocks, CHIPS, 0, 0, tiled=True)


def norm_kernel(tokens_ref, block_ref, normed_ref, copies_ref):
    normed_ref[...] = layer_norm(tokens_ref[...])[0].astype(bf16)
    copies_ref[...] = jnp.broadcast_to(block_ref[...][None], copies_ref.shape)


def norm_call(tokens, block, steps):
    rows, width = tokens.shape
    spec = pl.BlockSpec((rows // steps, width), lambda i: (i, 0))
    return pl.pallas_call(
        norm_kernel,
        grid=(steps,),
        in_specs=[spec, pl.BlockSpec(block.shape, lambda i: (0, 0))],
        out_specs=[spec, pl.BlockSpec((32 // steps,) + block.shape, lambda i: (i, 0, 0))],
        out_shape=[
            jax.ShapeDtypeStruct((rows, width), bf16),
            jax.ShapeDtypeStruct((32,) + block.shape, block.dtype),
        ],
        compiler_params=params(LIMIT),
        cost_estimate=cost(0, 1024),
    )(tokens, block)


def teacher_norm_kernel(tokens_ref, normed_ref):
    normed_ref[...] = layer_norm(tokens_ref[...])[0].astype(bf16)


def teacher_norm_call(tokens):
    spec = pl.BlockSpec(tokens.shape, lambda i: (0, 0))
    return pl.pallas_call(
        teacher_norm_kernel,
        grid=(1,),
        in_specs=[spec],
        out_specs=spec,
        out_shape=jax.ShapeDtypeStruct(tokens.shape, bf16),
        compiler_params=params(LIMIT),
        cost_estimate=cost(0, 1024),
    )(tokens)


LIMIT = 60
TILES = ((0, 512), (512, 512), (1024, 544))
PIECES = 4


def start_all(copies):
    for copy in copies:
        copy.start()
    return copies


def wait_all(copies):
    for copy in copies:
        copy.wait()


def store_delta(which_ref, hbm, vmem, sems):
    normed_hbm, weights_hbm, cotangent_hbm, delta_hbm = hbm
    normed_ref, weights_ref, cotangent_ref, delta_ref = vmem
    half = weights_ref.shape[1]
    columns = pl.ds(pl.multiple_of(which_ref[0] * half, half), half)
    weights_in = start_all([pltpu.make_async_copy(weights_hbm, weights_ref, sems.at[0])])
    tiles_in = []
    for n, (first, size) in enumerate(TILES):
        rows = pl.ds(first, size)
        tiles_in.append(
            start_all(
                [
                    pltpu.make_async_copy(
                        normed_hbm.at[rows], normed_ref.at[rows], sems.at[1 + 2 * n]
                    ),
                    pltpu.make_async_copy(
                        cotangent_hbm.at[rows, columns], cotangent_ref.at[rows], sems.at[2 + 2 * n]
                    ),
                ]
            )
        )
    out = []
    wait_all(weights_in)
    for n, (first, size) in enumerate(TILES):
        rows = pl.ds(first, size)
        wait_all(tiles_in[n])
        for m in range(0, half, 256):
            part = pl.ds(m, 256)
            preact = jnp.dot(normed_ref[rows, :], weights_ref[:, part], preferred_element_type=f32)
            slope = gelu_parts(preact)[1]
            delta_ref[rows, part] = (cotangent_ref[rows, part].astype(f32) * slope).astype(bf16)
        copy = pltpu.make_async_copy(delta_ref.at[rows], delta_hbm.at[rows], sems.at[7 + n])
        out += start_all([copy])
    return out


def gradient_piece(normed_ref, delta_ref, n, step):
    return lax.dot_general(
        normed_ref[:, n * step : (n + 1) * step],
        delta_ref[...],
        (((0,), (0,)), ((), ())),
        preferred_element_type=f32,
    )


def own_kernel(which_ref, normed_hbm, weights_hbm, cotangent_hbm, delta_hbm, *refs):
    sums_hbm, vmem, (sums_ref, sems) = refs[:PIECES], refs[PIECES:-2], refs[-2:]
    hbm = (normed_hbm, weights_hbm, cotangent_hbm, delta_hbm)
    out = store_delta(which_ref, hbm, vmem, sems)
    step = sums_ref.shape[0] // PIECES
    for n in range(PIECES):
        rows = pl.ds(n * step, step)
        sums_ref[rows, :] = gradient_piece(vmem[0], vmem[3], n, step).astype(bf16)
        copy = pltpu.make_async_copy(sums_ref.at[rows], sums_hbm[n], sems.at[10 + n])
        out += start_all([copy])
    wait_all(out)


def other_kernel(which_ref, normed_hbm, weights_hbm, cotangent_hbm, delta_hbm, *refs):
    hbm = (normed_hbm, weights_hbm, cotangent_hbm, delta_hbm)
    wait_all(store_delta(which_ref, hbm, refs[:-1], refs[-1]))


def sum_kernel(normed_hbm, delta_hbm, *refs):
    got_hbm, (sums_hbm, normed_ref, delta_ref, got_ref, sums_ref, sems) = refs[:PIECES], refs[PIECES:]
    step = sums_ref.shape[0] // PIECES
    delta_in = start_all([pltpu.make_async_copy(delta_hbm, delta_ref, sems.at[0])])
    pieces_in = []
    for n in range(PIECES):
        columns, rows = pl.ds(n * step, step), pl.ds(n * step, step)
        pieces_in.append(
            start_all(
                [
                    pltpu.make_async_copy(
                        normed_hbm.at[:, columns], normed_ref.at[:, columns], sems.at[1 + 2 * n]
                    ),
                    pltpu.make_async_copy(got_hbm[n], got_ref.at[rows], sems.at[2 + 2 * n]),
                ]
            )
        )
    out = []
    wait_all(delta_in)
    for n in range(PIECES):
        rows = pl.ds(n * step, step)
        wait_all(pieces_in[n])
        total = gradient_piece(normed_ref, delta_ref, n, step) + got_ref[rows, :].astype(f32)
        sums_ref[rows, :] = total.astype(bf16)
        copy = pltpu.make_async_copy(
            sums_ref.at[rows], sums_hbm.at[rows], sems.at[1 + 2 * PIECES + n]
        )
        out += start_all([copy])
    wait_all(out)


def local_call(kernel, outs, scratch, semaphores, *arrays):
    anywhere = pl.BlockSpec(memory_space=pl.ANY)
    return pl.pallas_call(
        kernel,
        in_specs=[
            pl.BlockSpec(memory_space=pltpu.SMEM) if array.ndim == 1 else anywhere
            for array in arrays
        ],
        out_specs=[anywhere] * len(outs),
        out_shape=[jax.ShapeDtypeStruct(shape, bf16) for shape in outs],
        scratch_shapes=[pltpu.VMEM(shape, bf16) for shape in scratch]
        + [pltpu.SemaphoreType.DMA((semaphores,))],
        compiler_params=params(LIMIT),
        cost_estimate=cost(0, 1024),
    )(*arrays)


def input_kernel(delta_own_ref, delta_other_ref, own_ref, other_ref, tokens_ref, out_ref):
    dims = (((1,), (1,)), ((), ()))
    back = lax.dot_general(delta_own_ref[...], own_ref[...], dims, preferred_element_type=f32)
    back += lax.dot_general(delta_other_ref[...], other_ref[...], dims, preferred_element_type=f32)
    centred, inv_std = layer_norm(tokens_ref[...])
    mean_back = jnp.mean(back, axis=-1, keepdims=True)
    mean_cross = jnp.mean(back * centred, axis=-1, keepdims=True)
    out_ref[...] = (inv_std * (back - mean_back - centred * mean_cross)).astype(bf16)


def input_call(delta_own, delta_other, own, other, tokens):
    rows, width = tokens.shape
    half = own.shape[1]
    deltas = pl.BlockSpec((784, half), lambda i: (i, 0))
    weights = pl.BlockSpec((width, half), lambda i: (0, 0))
    spec = pl.BlockSpec((784, width), lambda i: (i, 0))
    return pl.pallas_call(
        input_kernel,
        grid=(rows // 784,),
        in_specs=[deltas, deltas, weights, weights, spec],
        out_specs=spec,
        out_shape=jax.ShapeDtypeStruct((rows, width), bf16),
        compiler_params=params(LIMIT),
        cost_estimate=cost(4 * rows * width * half, 0),
    )(delta_own, delta_other, own, other, tokens)


def hidden_kernel(core_ref, normed_ref, own_ref, other_ref, hidden_ref):
    normed = normed_ref[...]
    half, step = own_ref.shape[1], 256
    for which, weights_ref in ((0, own_ref), (1, other_ref)):
        start = jnp.where(core_ref[0] == which, 0, half)
        for n in range(0, half, step):
            pre = jnp.dot(normed, weights_ref[:, n : n + step], preferred_element_type=f32)
            columns = pl.ds(pl.multiple_of(start + n, step), step)
            hidden_ref[:, columns] = gelu_parts(pre)[0].astype(bf16)


def hidden_call(normed, own, other, core):
    rows, width = normed.shape
    half, tile = own.shape[1], rows // 2
    weights = pl.BlockSpec((width, half), lambda i, core: (0, 0))
    return pl.pallas_call(
        hidden_kernel,
        grid_spec=pltpu.PrefetchScalarGridSpec(
            num_scalar_prefetch=1,
            grid=(rows // tile,),
            in_specs=[pl.BlockSpec((tile, width), lambda i, core: (i, 0)), weights, weights],
            out_specs=pl.BlockSpec((tile, 2 * half), lambda i, core: (i, 0)),
        ),
        out_shape=jax.ShapeDtypeStruct((rows, 2 * half), bf16),
        compiler_params=params(LIMIT),
        cost_estimate=cost(4 * rows * width * half, 0),
    )(core.astype(jnp.int32).reshape(1), normed, own, other)


def per_device(tokens, cotangent, global_tokens, master, first_moment, second_moment, teacher):
    core = lax.axis_index("core")

    width, half = tokens.shape[1], cotangent.shape[1] // 2

    copies = copies_of(half_block(master.astype(bf16), core))
    copies, tokens, global_tokens, teacher_rows = lax.optimization_barrier(
        (copies, tokens, global_tokens, teacher)
    )
    weights_own = exchanged(copies).reshape(width, half)
    teacher_block = half_block(teacher_rows.astype(bf16), core)
    normed, teacher_copies = norm_call(tokens, teacher_block, 2)
    teacher_normed = teacher_norm_call(global_tokens)
    normed, teacher_normed, teacher_copies, weights_own = lax.optimization_barrier(
        (normed, teacher_normed, teacher_copies, weights_own)
    )
    teacher_own = exchanged(teacher_copies).reshape(width, half)
    weights_other = swap(weights_own)

    rows = tokens.shape[0]
    delta, square = (rows, half), (width, half)
    vmem = [(rows, width), square, delta, delta]
    which = core.astype(jnp.int32).reshape(1)
    delta_own, *given = local_call(
        own_kernel,
        [delta] + [(width // PIECES, half)] * PIECES,
        vmem + [square],
        10 + PIECES,
        which,
        normed,
        weights_own,
        cotangent,
    )
    got = [swap(piece) for piece in given]
    (delta_other,) = local_call(
        other_kernel, [delta], vmem, 10, 1 - which, normed, weights_other, cotangent
    )
    (partial,) = local_call(
        sum_kernel,
        [square],
        [(rows, width), delta, square, square],
        1 + 3 * PIECES,
        normed,
        delta_other,
        *got,
    )
    pieces = exchanged(partial.reshape(32, 32, half))
    partial, delta_own, delta_other, teacher_own = lax.optimization_barrier(
        (partial, delta_own, delta_other, teacher_own)
    )
    grad_input = input_call(delta_own, delta_other, weights_own, weights_other, tokens)
    teacher_hidden = hidden_call(teacher_normed, teacher_own, swap(teacher_own), core)
    pieces, teacher_hidden, grad_input = lax.optimization_barrier(
        (pieces, teacher_hidden, grad_input)
    )
    group = jnp.sum(pieces.astype(f32), axis=0)
    group = lax.optimization_barrier(group.astype(bf16))
    mine = lax.dynamic_slice_in_dim(group, core * 16, 16, axis=0)
    other = lax.dynamic_slice_in_dim(group, (1 - core) * 16, 16, axis=0)
    here = mine.astype(f32) + lax.ppermute(mine, "yl", SWAP).astype(f32)
    diagonal = lax.ppermute(other, ("core", "yl"), [(0, 3), (1, 2), (2, 1), (3, 0)])
    there = swap(other).astype(f32) + diagonal.astype(f32)
    gradient = in_order(there, here, "core", 1)
    new_master, new_first, new_second, new_teacher = adamw_update(
        gradient, master, first_moment, second_moment, teacher
    )
    return (grad_input, teacher_hidden, new_master, new_first, new_second, new_teacher)


def solution(mesh):
    names = ("z", "x", "yh", "core", "yl")
    split = Mesh(mesh.devices.reshape(4, 4, 2, 2, 2), names)
    tokens = P(names, None)
    rows = P(names[:-1], None)
    return jax.shard_map(
        per_device,
        mesh=split,
        in_specs=(tokens, tokens, tokens, rows, rows, rows, rows),
        out_specs=(tokens, tokens, rows, rows, rows, rows),
        check_vma=False,
    )
```

time: 210 us -> 135 us (0.64)
  blocking collectives: 74.5 us -> 0 us
  Pallas kernels: 0 us -> 60.3 us
  matrix products: 42.7 us -> 0 us
  starting transfers between devices: 6.83 us -> 35.1 us
  waiting for transfers between devices: 57.4 us -> 32.4 us
  between operations: 14.2 us -> 0.85 us
  other arithmetic: 14 us -> 2.84 us
  local copies, waits for them, and re-layouts: 0.33 us -> 2.75 us
    all_to_all x2 -> x0, blocking collectives: 74.5 us -> none  [the longest x1 40.4 us: per_device(): weights_own = lax.all_to_all(copies, CHIPS, 0, 0, tiled=True)]
    pallas_call x0 -> x7, Pallas kernels: none -> 60.3 us  [the longest x3 29.7 us: local_call(): pl.pallas_call(kernel, in_specs=[pl.BlockSpec(memory_space=pltpu.SMEM) if...]
    all_gather x1 -> x0, waiting for transfers between devices: 50.5 us -> none  [per_device(): lax.all_gather(teacher.astype(bf16), ('z', 'x', 'yh', 'core'), axis=0, ti...]
    dot_general x7 -> x0, matrix products: 42.7 us -> none  [the longest x2 15 us: delta_of(): preact = jnp.dot(normed, weights, preferred_element_type=f32)]
    all_to_all x0 -> x3, waiting for transfers between devices: none -> 29.2 us  [exchanged(): return lax.all_to_all(blocks, CHIPS, 0, 0, tiled=True)]
    all_to_all x0 -> x3, starting transfers between devices: none -> 25.2 us  [exchanged(): return lax.all_to_all(blocks, CHIPS, 0, 0, tiled=True)]
    reduce_sum x5 -> x1, other arithmetic: 7.2 us -> 0.38 us  [per_device(): group = jnp.sum(pieces.astype(f32), axis=0)]
    convert_element_type x2, other arithmetic: 4.07 us -> 0.92 us  [the longest x1 0.91 us: per_device(): copies = copies_of(half_block(master.astype(bf16), core))]
  transfers between devices with their start and end apart: 6 -> 14, of which waited for: 5 -> 4; matrix products, arithmetic and copies ran while one was open for 13% -> 1% of each run, Pallas kernels for 0% -> 45%
where the time goes in v3:
time: 135 us; the launch traced here: 134 us
  Pallas kernels  60.3 us (45%)
  starting transfers between devices  35.1 us (26%)
  waiting for transfers between devices  32.4 us (24%)
  other arithmetic  2.84 us (2%)
  local copies, waits for them, and re-layouts  2.75 us (2%)
    pallas_call x3, Pallas kernels, local_call(): pl.pallas_call(kernel, in_specs=[pl.BlockSpec(memory_space=pltpu.SMEM) if...  29.7 us
    all_to_all x3, waiting for transfers between devices, exchanged(): return lax.all_to_all(blocks, CHIPS, 0, 0, tiled=True)  29.2 us
    all_to_all x3, starting transfers between devices, exchanged(): return lax.all_to_all(blocks, CHIPS, 0, 0, tiled=True)  25.2 us
    pallas_call x1, Pallas kernels, input_call(): pl.pallas_call(input_kernel, grid=(rows // 784,), in_specs=[deltas, delta...  14.3 us
    ppermute x9, starting transfers between devices, swap(): return lax.ppermute(block, 'core', SWAP)  8.47 us
    pallas_call x1, Pallas kernels, hidden_call(): pl.pallas_call(hidden_kernel, grid_spec=pltpu.PrefetchScalarGridSpec(num_...  7.89 us
    pallas_call x1, Pallas kernels, norm_call(): pl.pallas_call(norm_kernel, grid=(steps,), in_specs=[spec, pl.BlockSpec(b...  4.9 us
    pallas_call x1, Pallas kernels, teacher_norm_call(): pl.pallas_call(teacher_norm_kernel, grid=(1,), in_specs=[spec], out_specs...  3.55 us
  transfers between devices with their start and end apart: 14, of which 4 were waited for; matrix products, arithmetic and copies ran while one was open for 1% of the time, Pallas kernels for 45%

profile of v3, /device:TPU:1, one launch (start us, length us, event | category | flops | bytes accessed | tf_op | source)
XLA Modules:
  0.0 134.3 jit_solution(6611964041174958079)
XLA Ops:
  0.6 0.9 convert_element_type.20
  1.6 1.5 %collective-permute-start = (bf16[16,1024]{1,0:T(8,128)(2,1)S(1)}, bf16[16,1024]{1,0:T(8,128)(2,1)S(1)}, u32[]{:S(2)}, u32[]{:S(2)}) collective-permute-start(bf16[16,1024]{1,0:T(8,128)(2,1)S(1)} %get-tuple-element.57), channel_id=1, source_target_pairs={{0,2},{2,0},{1,3},{3,1},{4,6},{6,4},{5,7},{7,5},{8,10},{10,8},{9,1... | collective-permute-start | bytes 98312 | tf_op jit(solution)/shard_map/ppermute | solution.py:58
  3.1 0.9 collective-permute-done
  3.9 1.6 %broadcast_in_dim.2 = bf16[32,32,1024]{2,1,0:T(8,128)(2,1)} broadcast(bf16[32,1024]{1,0:T(8,128)(2,1)S(1)} %maximum_select_fusion.1), dimensions={1,2} | broadcast | bytes 2162688 | tf_op jit(solution)/shard_map/broadcast_in_dim | solution.py:80
  5.5 10.7 %all-to-all-start = ((bf16[32,32,1024]{2,1,0:T(8,128)(2,1)}), bf16[32,32,1024]{2,1,0:T(8,128)(2,1)S(1)}, u32[]{:S(2)}, u32[]{:S(2)}) async-start(bf16[32,32,1024]{2,1,0:T(8,128)(2,1)} %broadcast_in_dim.2), calls=%async_computation | async-start | bytes 4194304 | tf_op jit(solution)/shard_map/all_to_all | solution.py:84
  16.3 0.7 collective-permute-start.1
  17.0 3.6 %shard_map.119.normed_ref = bf16[784,1024]{1,0:T(8,128)(2,1)} custom-call(bf16[784,1024]{1,0:T(8,128)(2,1)} %tokens_ref.1), custom_call_target="tpu_custom_call" | custom-call | bytes 1024 | tf_op jit(solution)/shard_map/pallas_call | solution.py:115
  21.2 4.9 %shard_map.118 = (bf16[1568,1024]{1,0:T(8,128)(2,1)}, bf16[32,32,1024]{2,1,0:T(8,128)(2,1)}) custom-call(bf16[1568,1024]{1,0:T(8,128)(2,1)} %tokens_ref.2, bf16[32,1024]{1,0:T(8,128)(2,1)} %maximum_select_fusion.2.block_ref), custom_call_target="tpu_custom_call" | custom-call | bytes 1024 | tf_op jit(solution)/shard_map/pallas_call | solution.py:95
  26.1 20.9 %all-to-all-done = bf16[32,32,1024]{2,1,0:T(8,128)(2,1)S(1)} async-done(((bf16[32,32,1024]{2,1,0:T(8,128)(2,1)}), bf16[32,32,1024]{2,1,0:T(8,128)(2,1)S(1)}, u32[]{:S(2)}, u32[]{:S(2)}) %all-to-all-start) | async-done | bytes 2097184 | tf_op jit(solution)/shard_map/all_to_all | solution.py:84
  47.0 1.7 %collective-permute-start.2 = (bf16[1024,1024]{1,0:T(8,128)(2,1)S(1)}, bf16[1024,1024]{1,0:T(8,128)(2,1)}, u32[]{:S(2)}, u32[]{:S(2)}) collective-permute-start(bf16[1024,1024]{1,0:T(8,128)(2,1)S(1)} %bitcast.4), channel_id=1, source_target_pairs={{0,2},{2,0},{1,3},{3,1},{4,6},{6,4},{5,7},{7,5},{8,10},{10,8},{9,1... | collective-permute-start | bytes 6291464 | tf_op jit(solution)/shard_map/ppermute | solution.py:58
  48.8 4.8 %all-to-all-start.2 = ((bf16[32,32,1024]{2,1,0:T(8,128)(2,1)}), bf16[32,32,1024]{2,1,0:T(8,128)(2,1)}, u32[]{:S(2)}, u32[]{:S(2)}) async-start(bf16[32,32,1024]{2,1,0:T(8,128)(2,1)} %get-tuple-element.41), calls=%async_computation.2 | async-start | bytes 4194304 | tf_op jit(solution)/shard_map/all_to_all | solution.py:84
  53.6 12.7 %shard_map.121 = (bf16[1568,1024]{1,0:T(8,128)(2,1)}, bf16[256,1024]{1,0:T(8,128)(2,1)}, bf16[256,1024]{1,0:T(8,128)(2,1)}, bf16[256,1024]{1,0:T(8,128)(2,1)}, bf16[256,1024]{1,0:T(8,128)(2,1)}) custom-call(s32[1]{0:T(128)} %bitcast.1.which_ref.core_ref, bf16[1568,1024]{1,0:T(8,128)(2,1)} %get-tuple-element.33.normed_hbm, bf16[1024,1024]{1,0:T(8,128)(2,1)} %bitcast.5, ...), custom_call_target="tpu_custom_call" | custom-call | bytes 1024 | tf_op jit(solution)/shard_map/pallas_call | solution.py:238
  66.3 1.4 %collective-permute-start.3 = (bf16[256,1024]{1,0:T(8,128)(2,1)}, bf16[256,1024]{1,0:T(8,128)(2,1)S(1)}, u32[]{:S(2)}, u32[]{:S(2)}) collective-permute-start(bf16[256,1024]{1,0:T(8,128)(2,1)} %get-tuple-element.35), channel_id=1, source_target_pairs={{0,2},{2,0},{1,3},{3,1},{4,6},{6,4},{5,7},{7,5},{8,10},{10,8},{9,1... | collective-permute-start | bytes 1572872 | tf_op jit(solution)/shard_map/ppermute | solution.py:58
  68.5 9.1 %shard_map.120.delta_hbm.delta_other_ref = bf16[1568,1024]{1,0:T(8,128)(2,1)} custom-call(s32[1]{0:T(128)S(6)} %sub.12.which_ref, bf16[1568,1024]{1,0:T(8,128)(2,1)} %get-tuple-element.33.normed_hbm, bf16[1024,1024]{1,0:T(8,128)(2,1)} %collective-permute-done.2.weights_hbm.other_ref, bf16[1568,2048]{1,0:T(8,128)(2,1)} %cotangent_hbm.3), custom_call_target="tpu_custom_call" | custom-call | bytes 1024 | tf_op jit(solution)/shard_map/pallas_call | solution.py:238
  77.8 0.7 copy-done.3
  78.8 7.8 %shard_map.122 = bf16[1024,1024]{1,0:T(8,128)(2,1)} custom-call(bf16[1568,1024]{1,0:T(8,128)(2,1)} %get-tuple-element.33.normed_hbm, bf16[1568,1024]{1,0:T(8,128)(2,1)} %shard_map.120.delta_hbm.delta_other_ref, bf16[256,1024]{1,0:T(8,128)(2,1)} %copy-done.3, bf16[256,1024]{1,0:T(8,128)(2,1)} %copy-done.4, bf16[256,1024]{1,0:T(8,128)(2,1)} %copy-done.5, ...), custom_call_target="tpu_custom_call" | custom-call | bytes 1024 | tf_op jit(solution)/shard_map/pallas_call | solution.py:238
  87.0 9.7 %all-to-all-start.1 = ((bf16[32,32,1024]{2,1,0:T(8,128)(2,1)}), bf16[32,32,1024]{2,1,0:T(8,128)(2,1)S(1)}, u32[]{:S(2)}, u32[]{:S(2)}) async-start(bf16[32,32,1024]{2,1,0:T(8,128)(2,1)} %bitcast.7), calls=%async_computation.1 | async-start | bytes 4194304 | tf_op jit(solution)/shard_map/all_to_all | solution.py:84
  96.7 14.3 %shard_map.124 = bf16[1568,1024]{1,0:T(8,128)(2,1)} custom-call(bf16[1568,1024]{1,0:T(8,128)(2,1)} %get-tuple-element.43.delta_own_ref, bf16[1568,1024]{1,0:T(8,128)(2,1)} %shard_map.120.delta_hbm.delta_other_ref, bf16[1024,1024]{1,0:T(8,128)(2,1)} %bitcast.6, bf16[1024,1024]{1,0:T(8,128)(2,1)} %collective-permute-done.2.weights_hbm.other_ref, ...), custom_call_target="tpu_custom_call" | custom-call | flops 6576668672 | tf_op jit(solution)/shard_map/pallas_call | solution.py:269
  110.9 7.9 %shard_map.123 = bf16[784,2048]{1,0:T(8,128)(2,1)} custom-call(s32[1]{0:T(128)} %bitcast.1.which_ref.core_ref, bf16[784,1024]{1,0:T(8,128)(2,1)} %shard_map.119.normed_ref, bf16[1024,1024]{1,0:T(8,128)(2,1)} %bitcast.3.own_ref, bf16[1024,1024]{1,0:T(8,128)(2,1)} %collective-permute-done.7.other_ref), custom_call_target="tpu_custom_call" | custom-call | flops 3288334336 | tf_op jit(solution)/shard_map/pallas_call | solution.py:295
  118.8 8.3 %all-to-all-done.1 = bf16[32,32,1024]{2,1,0:T(8,128)(2,1)S(1)} async-done(((bf16[32,32,1024]{2,1,0:T(8,128)(2,1)}), bf16[32,32,1024]{2,1,0:T(8,128)(2,1)S(1)}, u32[]{:S(2)}, u32[]{:S(2)}) %all-to-all-start.1) | async-done | bytes 2097184 | tf_op jit(solution)/shard_map/all_to_all | solution.py:84
  128.1 2.0 %collective-permute-start.8 = (bf16[16,1024]{1,0:T(8,128)(2,1)S(1)}, bf16[16,1024]{1,0:T(8,128)(2,1)S(1)}, u32[]{:S(2)}, u32[]{:S(2)}) collective-permute-start(bf16[16,1024]{1,0:T(8,128)(2,1)S(1)} %get-tuple-element.53), channel_id=1, source_target_pairs={{0,2},{2,0},{1,3},{3,1},{4,6},{6,4},{5,7},{7,5},{8,10},{10,8},{9,1... | collective-permute-start | bytes 98312 | tf_op jit(solution)/shard_map/ppermute | solution.py:58
  130.0 1.0 collective-permute-start.9
  131.0 2.4 %collective-permute-done.9 = bf16[16,1024]{1,0:T(8,128)(2,1)S(1)} collective-permute-done((bf16[16,1024]{1,0:T(8,128)(2,1)S(1)}, bf16[16,1024]{1,0:T(8,128)(2,1)S(1)}, u32[]{:S(2)}, u32[]{:S(2)}) %collective-permute-start.9) | collective-permute-done | bytes 32800 | tf_op jit(solution)/shard_map/ppermute | solution.py:369
  133.4 0.9 multiply_add_fusion
  (39 shorter events, 3.1 us)
Async XLA Ops:
  1.6 2.4 %collective-permute-start = (bf16[16,1024]{1,0:T(8,128)(2,1)S(1)}, bf16[16,1024]{1,0:T(8,128)(2,1)S(1)}, u32[]{:S(2)}, u32[]{:S(2)}) collective-permute-start(bf16[16,1024]{1,0:T(8,128)(2,1)S(1)} %get-tuple-element.57), channel_id=1, source_target_pairs={{0,2},{2,0},{1,3},{3,1},{4,6},{6,4},{5,7},{7,5},{8,10},{10,8},{9,1... | collective-permute-start | bytes 98312 | tf_op jit(solution)/shard_map/ppermute | solution.py:58
  5.5 10.7 %copy-start.1 = (f32[16,2048]{1,0:T(8,128)S(1)}, f32[16,2048]{1,0:T(8,128)}, u32[]{:S(2)}) copy-start(f32[16,2048]{1,0:T(8,128)} %param.13) | copy-start | bytes 393220
  5.5 41.5 %all-to-all-start = ((bf16[32,32,1024]{2,1,0:T(8,128)(2,1)}), bf16[32,32,1024]{2,1,0:T(8,128)(2,1)S(1)}, u32[]{:S(2)}, u32[]{:S(2)}) async-start(bf16[32,32,1024]{2,1,0:T(8,128)(2,1)} %broadcast_in_dim.2), calls=%async_computation | async-start | bytes 4194304 | tf_op jit(solution)/shard_map/all_to_all | solution.py:84
  16.3 4.3 %collective-permute-start.1 = (bf16[16,1024]{1,0:T(8,128)(2,1)S(1)}, bf16[16,1024]{1,0:T(8,128)(2,1)S(1)}, u32[]{:S(2)}, u32[]{:S(2)}) collective-permute-start(bf16[16,1024]{1,0:T(8,128)(2,1)S(1)} %get-tuple-element.55), channel_id=1, source_target_pairs={{0,2},{2,0},{1,3},{3,1},{4,6},{6,4},{5,7},{7,5},{8,10},{10,8},{9,1... | collective-permute-start | bytes 98312 | tf_op jit(solution)/shard_map/ppermute | solution.py:58
  47.0 1.8 %copy-start = (bf16[32,32,1024]{2,1,0:T(8,128)(2,1)}, bf16[32,32,1024]{2,1,0:T(8,128)(2,1)S(1)}, u32[]{:S(2)}) copy-start(bf16[32,32,1024]{2,1,0:T(8,128)(2,1)S(1)} %all-to-all-done) | copy-start | bytes 6291460
  47.0 21.5 %collective-permute-start.2 = (bf16[1024,1024]{1,0:T(8,128)(2,1)S(1)}, bf16[1024,1024]{1,0:T(8,128)(2,1)}, u32[]{:S(2)}, u32[]{:S(2)}) collective-permute-start(bf16[1024,1024]{1,0:T(8,128)(2,1)S(1)} %bitcast.4), channel_id=1, source_target_pairs={{0,2},{2,0},{1,3},{3,1},{4,6},{6,4},{5,7},{7,5},{8,10},{10,8},{9,1... | collective-permute-start | bytes 6291464 | tf_op jit(solution)/shard_map/ppermute | solution.py:58
  48.8 37.9 %all-to-all-start.2 = ((bf16[32,32,1024]{2,1,0:T(8,128)(2,1)}), bf16[32,32,1024]{2,1,0:T(8,128)(2,1)}, u32[]{:S(2)}, u32[]{:S(2)}) async-start(bf16[32,32,1024]{2,1,0:T(8,128)(2,1)} %get-tuple-element.41), calls=%async_computation.2 | async-start | bytes 4194304 | tf_op jit(solution)/shard_map/all_to_all | solution.py:84
  66.3 11.4 %collective-permute-start.3 = (bf16[256,1024]{1,0:T(8,128)(2,1)}, bf16[256,1024]{1,0:T(8,128)(2,1)S(1)}, u32[]{:S(2)}, u32[]{:S(2)}) collective-permute-start(bf16[256,1024]{1,0:T(8,128)(2,1)} %get-tuple-element.35), channel_id=1, source_target_pairs={{0,2},{2,0},{1,3},{3,1},{4,6},{6,4},{5,7},{7,5},{8,10},{10,8},{9,1... | collective-permute-start | bytes 1572872 | tf_op jit(solution)/shard_map/ppermute | solution.py:58
  67.8 9.9 %collective-permute-start.4 = (bf16[256,1024]{1,0:T(8,128)(2,1)}, bf16[256,1024]{1,0:T(8,128)(2,1)S(1)}, u32[]{:S(2)}, u32[]{:S(2)}) collective-permute-start(bf16[256,1024]{1,0:T(8,128)(2,1)} %get-tuple-element.36), channel_id=1, source_target_pairs={{0,2},{2,0},{1,3},{3,1},{4,6},{6,4},{5,7},{7,5},{8,10},{10,8},{9,1... | collective-permute-start | bytes 1572872 | tf_op jit(solution)/shard_map/ppermute | solution.py:58
  68.0 9.7 %collective-permute-start.5 = (bf16[256,1024]{1,0:T(8,128)(2,1)}, bf16[256,1024]{1,0:T(8,128)(2,1)S(1)}, u32[]{:S(2)}, u32[]{:S(2)}) collective-permute-start(bf16[256,1024]{1,0:T(8,128)(2,1)} %get-tuple-element.37), channel_id=1, source_target_pairs={{0,2},{2,0},{1,3},{3,1},{4,6},{6,4},{5,7},{7,5},{8,10},{10,8},{9,1... | collective-permute-start | bytes 1572872 | tf_op jit(solution)/shard_map/ppermute | solution.py:58
  68.3 9.5 %collective-permute-start.6 = (bf16[256,1024]{1,0:T(8,128)(2,1)}, bf16[256,1024]{1,0:T(8,128)(2,1)}, u32[]{:S(2)}, u32[]{:S(2)}) collective-permute-start(bf16[256,1024]{1,0:T(8,128)(2,1)} %get-tuple-element.38), channel_id=1, source_target_pairs={{0,2},{2,0},{1,3},{3,1},{4,6},{6,4},{5,7},{7,5},{8,10},{10,8},{9,1... | collective-permute-start | bytes 1572872 | tf_op jit(solution)/shard_map/ppermute | solution.py:58
  77.7 0.8 copy-start.3
  77.7 1.0 copy-start.4
  77.7 1.1 copy-start.5
  86.7 24.3 %collective-permute-start.7 = (bf16[1024,1024]{1,0:T(8,128)(2,1)}, bf16[1024,1024]{1,0:T(8,128)(2,1)}, u32[]{:S(2)}, u32[]{:S(2)}) collective-permute-start(bf16[1024,1024]{1,0:T(8,128)(2,1)} %bitcast.3.own_ref), channel_id=1, source_target_pairs={{0,2},{2,0},{1,3},{3,1},{4,6},{6,4},{5,7},{7,5},{8,10},{10,8},{9,1... | collective-permute-start | bytes 6291464 | tf_op jit(solution)/shard_map/ppermute | solution.py:58
  87.0 40.2 %all-to-all-start.1 = ((bf16[32,32,1024]{2,1,0:T(8,128)(2,1)}), bf16[32,32,1024]{2,1,0:T(8,128)(2,1)S(1)}, u32[]{:S(2)}, u32[]{:S(2)}) async-start(bf16[32,32,1024]{2,1,0:T(8,128)(2,1)} %bitcast.7), calls=%async_computation.1 | async-start | bytes 4194304 | tf_op jit(solution)/shard_map/all_to_all | solution.py:84
  118.8 14.5 %copy-start.2 = (f32[16,2048]{1,0:T(8,128)S(1)}, f32[16,2048]{1,0:T(8,128)}, u32[]{:S(2)}) copy-start(f32[16,2048]{1,0:T(8,128)} %param.10) | copy-start | bytes 393220
  118.8 14.5 %copy-start.6 = (f32[16,2048]{1,0:T(8,128)S(1)}, f32[16,2048]{1,0:T(8,128)}, u32[]{:S(2)}) copy-start(f32[16,2048]{1,0:T(8,128)} %param.11) | copy-start | bytes 393220
  118.8 14.5 %copy-start.7 = (f32[16,2048]{1,0:T(8,128)S(1)}, f32[16,2048]{1,0:T(8,128)}, u32[]{:S(2)}) copy-start(f32[16,2048]{1,0:T(8,128)} %param.12) | copy-start | bytes 393220
  127.6 3.4 %collective-permute-start.10 = (bf16[16,1024]{1,0:T(8,128)(2,1)S(1)}, bf16[16,1024]{1,0:T(8,128)(2,1)S(1)}, u32[]{:S(2)}, u32[]{:S(2)}) collective-permute-start(bf16[16,1024]{1,0:T(8,128)(2,1)S(1)} %get-tuple-element.52), channel_id=1, source_target_pairs={{0,1},{1,0},{2,3},{3,2},{4,5},{5,4},{6,7},{7,6},{8,9},{9,8},{10,11... | collective-permute-start | bytes 98312 | tf_op jit(solution)/shard_map/ppermute | solution.py:368
  128.1 2.9 %collective-permute-start.8 = (bf16[16,1024]{1,0:T(8,128)(2,1)S(1)}, bf16[16,1024]{1,0:T(8,128)(2,1)S(1)}, u32[]{:S(2)}, u32[]{:S(2)}) collective-permute-start(bf16[16,1024]{1,0:T(8,128)(2,1)S(1)} %get-tuple-element.53), channel_id=1, source_target_pairs={{0,2},{2,0},{1,3},{3,1},{4,6},{6,4},{5,7},{7,5},{8,10},{10,8},{9,1... | collective-permute-start | bytes 98312 | tf_op jit(solution)/shard_map/ppermute | solution.py:58
  130.0 3.3 %collective-permute-start.9 = (bf16[16,1024]{1,0:T(8,128)(2,1)S(1)}, bf16[16,1024]{1,0:T(8,128)(2,1)S(1)}, u32[]{:S(2)}, u32[]{:S(2)}) collective-permute-start(bf16[16,1024]{1,0:T(8,128)(2,1)S(1)} %get-tuple-element.53), channel_id=1, source_target_pairs={{0,3},{1,2},{2,1},{3,0},{4,7},{5,6},{6,5},{7,4},{8,11},{9,10},{10,... | collective-permute-start | bytes 98312 | tf_op jit(solution)/shard_map/ppermute | solution.py:369

commit v4 on v3

--- a/solution.py
+++ b/solution.py
@@ -19,6 +19,7 @@
 bias_two = 0.09520785288629038
 
 SWAP = [(0, 1), (1, 0)]
+ACROSS = [(0, 3), (3, 0), (1, 2), (2, 1)]
 CHIPS = ("z", "x", "yh")
 bf16, f32 = jnp.bfloat16, jnp.float32
 
@@ -80,41 +81,36 @@
     return jnp.broadcast_to(block[None], (32,) + block.shape)
 
 
-def exchanged(blocks):
-    return lax.all_to_all(blocks, CHIPS, 0, 0, tiled=True)
-
-
-def norm_kernel(tokens_ref, block_ref, normed_ref, copies_ref):
+def exchanged(blocks, chips=CHIPS):
+    return lax.all_to_all(blocks, chips, 0, 0, tiled=True)
+
+
+def copies_kernel(block_ref, copies_ref):
+    copies_ref[...] = jnp.broadcast_to(block_ref[...][None], copies_ref.shape)
+
+
+def copies_call(block, count, steps):
+    return pl.pallas_call(
+        copies_kernel,
+        grid=(steps,),
+        in_specs=[pl.BlockSpec(block.shape, lambda i: (0, 0))],
+        out_specs=pl.BlockSpec((count // steps,) + block.shape, lambda i: (i, 0, 0)),
+        out_shape=jax.ShapeDtypeStruct((count,) + block.shape, block.dtype),
+        compiler_params=params(LIMIT),
+        cost_estimate=cost(0, 1024),
+    )(block)
+
+
+def norm_kernel(tokens_ref, normed_ref):
     normed_ref[...] = layer_norm(tokens_ref[...])[0].astype(bf16)
-    copies_ref[...] = jnp.broadcast_to(block_ref[...][None], copies_ref.shape)
-
-
-def norm_call(tokens, block, steps):
+
+
+def norm_call(tokens, steps):
     rows, width = tokens.shape
     spec = pl.BlockSpec((rows // steps, width), lambda i: (i, 0))
     return pl.pallas_call(
         norm_kernel,
         grid=(steps,),
-        in_specs=[spec, pl.BlockSpec(block.shape, lambda i: (0, 0))],
-        out_specs=[spec, pl.BlockSpec((32 // steps,) + block.shape, lambda i: (i, 0, 0))],
-        out_shape=[
-            jax.ShapeDtypeStruct((rows, width), bf16),
-            jax.ShapeDtypeStruct((32,) + block.shape, block.dtype),
-        ],
-        compiler_params=params(LIMIT),
-        cost_estimate=cost(0, 1024),
-    )(tokens, block)
-
-
-def teacher_norm_kernel(tokens_ref, normed_ref):
-    normed_ref[...] = layer_norm(tokens_ref[...])[0].astype(bf16)
-
-
-def teacher_norm_call(tokens):
-    spec = pl.BlockSpec(tokens.shape, lambda i: (0, 0))
-    return pl.pallas_call(
-        teacher_norm_kernel,
-        grid=(1,),
         in_specs=[spec],
         out_specs=spec,
         out_shape=jax.ShapeDtypeStruct(tokens.shape, bf16),
@@ -123,7 +119,7 @@
     )(tokens)
 
 
-LIMIT = 60
+LIMIT = 62
 TILES = ((0, 512), (512, 512), (1024, 544))
 PIECES = 4
 
@@ -272,7 +268,7 @@
         in_specs=[deltas, deltas, weights, weights, spec],
         out_specs=spec,
         out_shape=jax.ShapeDtypeStruct((rows, width), bf16),
-        compiler_params=params(LIMIT),
+        compiler_params=params(60),
         cost_estimate=cost(4 * rows * width * half, 0),
     )(delta_own, delta_other, own, other, tokens)
 
@@ -290,7 +286,7 @@
 
 def hidden_call(normed, own, other, core):
     rows, width = normed.shape
-    half, tile = own.shape[1], rows // 2
+    half, tile = own.shape[1], rows
     weights = pl.BlockSpec((width, half), lambda i, core: (0, 0))
     return pl.pallas_call(
         hidden_kernel,
@@ -301,7 +297,7 @@
             out_specs=pl.BlockSpec((tile, 2 * half), lambda i, core: (i, 0)),
         ),
         out_shape=jax.ShapeDtypeStruct((rows, 2 * half), bf16),
-        compiler_params=params(LIMIT),
+        compiler_params=params(60),
         cost_estimate=cost(4 * rows * width * half, 0),
     )(core.astype(jnp.int32).reshape(1), normed, own, other)
 
@@ -317,12 +313,14 @@
     )
     weights_own = exchanged(copies).reshape(width, half)
     teacher_block = half_block(teacher_rows.astype(bf16), core)
-    normed, teacher_copies = norm_call(tokens, teacher_block, 2)
-    teacher_normed = teacher_norm_call(global_tokens)
+    beyond = lax.ppermute(teacher_block, ("yh", "yl"), ACROSS)
+    teacher_block = in_order(teacher_block, beyond, "yh", 0)
+    teacher_copies = copies_call(teacher_block, 16, 1)
+    normed, teacher_normed = norm_call(tokens, 2), norm_call(global_tokens, 1)
     normed, teacher_normed, teacher_copies, weights_own = lax.optimization_barrier(
         (normed, teacher_normed, teacher_copies, weights_own)
     )
-    teacher_own = exchanged(teacher_copies).reshape(width, half)
+    teacher_own = exchanged(teacher_copies, ("z", "x")).reshape(width, half)
     weights_other = swap(weights_own)
 
     rows = tokens.shape[0]

time: 135 us -> 132 us (0.978)
  waiting for transfers between devices: 32.4 us -> 28.9 us
  Pallas kernels: 60.3 us -> 62.6 us
    all_to_all x3, waiting for transfers between devices: 29.2 us -> 11.5 us  [exchanged(): return lax.all_to_all(blocks, chips, 0, 0, tiled=True)]
    ppermute x0 -> x1, waiting for transfers between devices: none -> 13.3 us  [per_device(): beyond = lax.ppermute(teacher_block, ('yh', 'yl'), ACROSS)]
    all_to_all x3, starting transfers between devices: 25.2 us -> 21.6 us  [exchanged(): return lax.all_to_all(blocks, chips, 0, 0, tiled=True)]
    ppermute x0 -> x1, starting transfers between devices: none -> 2.84 us  [per_device(): beyond = lax.ppermute(teacher_block, ('yh', 'yl'), ACROSS)]
    ppermute x9, starting transfers between devices: 8.47 us -> 6.38 us  [swap(): return lax.ppermute(block, 'core', SWAP)]
    pallas_call x2 -> x3, Pallas kernels: 8.45 us -> 10.4 us  [the longest x2 8.01 us: norm_call(): pl.pallas_call(norm_kernel, grid=(steps,), in_specs=[spec], out_specs=spe...]
    ppermute x1, starting transfers between devices: 0.96 us -> 2.7 us  [per_device(): lax.ppermute(other, ('core', 'yl'), [(0, 3), (1, 2), (2, 1), (3, 0)])]
  transfers between devices with their start and end apart: 14 -> 15, of which waited for: 4 -> 7; matrix products, arithmetic and copies ran while one was open for 1% -> 1% of each run, Pallas kernels for 45% -> 47%
where the time goes in v4:
time: 132 us
  Pallas kernels  62.6 us (47%)
  starting transfers between devices  34 us (26%)
  waiting for transfers between devices  28.9 us (22%)
  other arithmetic  2.89 us (2%)
  local copies, waits for them, and re-layouts  2.72 us (2%)
    pallas_call x3, Pallas kernels, local_call(): pl.pallas_call(kernel, in_specs=[pl.BlockSpec(memory_space=pltpu.SMEM) if...  29.7 us
    all_to_all x3, starting transfers between devices, exchanged(): return lax.all_to_all(blocks, chips, 0, 0, tiled=True)  21.6 us
    pallas_call x1, Pallas kernels, input_call(): pl.pallas_call(input_kernel, grid=(rows // 784,), in_specs=[deltas, delta...  14.3 us
    ppermute x1, waiting for transfers between devices, per_device(): beyond = lax.ppermute(teacher_block, ('yh', 'yl'), ACROSS)  13.3 us
    all_to_all x3, waiting for transfers between devices, exchanged(): return lax.all_to_all(blocks, chips, 0, 0, tiled=True)  11.5 us
    pallas_call x1, Pallas kernels, hidden_call(): pl.pallas_call(hidden_kernel, grid_spec=pltpu.PrefetchScalarGridSpec(num_...  8.22 us
    pallas_call x2, Pallas kernels, norm_call(): pl.pallas_call(norm_kernel, grid=(steps,), in_specs=[spec], out_specs=spe...  8.01 us
    ppermute x9, starting transfers between devices, swap(): return lax.ppermute(block, 'core', SWAP)  6.38 us
  transfers between devices with their start and end apart: 15, of which 7 were waited for; matrix products, arithmetic and copies ran while one was open for 1% of the time, Pallas kernels for 47%

profile of v4, /device:TPU:1, one launch (start us, length us, event | category | flops | bytes accessed | tf_op | source)
XLA Modules:
  0.0 131.9 jit_solution(12222808826860472999)
XLA Ops:
  0.6 0.9 convert_element_type.20
  1.6 1.5 %collective-permute-start = (bf16[16,1024]{1,0:T(8,128)(2,1)S(1)}, bf16[16,1024]{1,0:T(8,128)(2,1)S(1)}, u32[]{:S(2)}, u32[]{:S(2)}) collective-permute-start(bf16[16,1024]{1,0:T(8,128)(2,1)S(1)} %get-tuple-element.53), channel_id=1, source_target_pairs={{0,2},{2,0},{1,3},{3,1},{4,6},{6,4},{5,7},{7,5},{8,10},{10,8},{9,1... | collective-permute-start | bytes 98312 | tf_op jit(solution)/shard_map/ppermute | solution.py:59
  3.1 0.9 collective-permute-done
  3.9 1.6 %broadcast_in_dim.2 = bf16[32,32,1024]{2,1,0:T(8,128)(2,1)} broadcast(bf16[32,1024]{1,0:T(8,128)(2,1)S(1)} %maximum_select_fusion.2), dimensions={1,2} | broadcast | bytes 2162688 | tf_op jit(solution)/shard_map/broadcast_in_dim | solution.py:81
  5.5 10.9 %all-to-all-start = ((bf16[32,32,1024]{2,1,0:T(8,128)(2,1)}), bf16[32,32,1024]{2,1,0:T(8,128)(2,1)}, u32[]{:S(2)}, u32[]{:S(2)}) async-start(bf16[32,32,1024]{2,1,0:T(8,128)(2,1)} %broadcast_in_dim.2), calls=%async_computation | async-start | bytes 4194304 | tf_op jit(solution)/shard_map/all_to_all | solution.py:85
  18.0 2.8 %collective-permute-start.2 = (bf16[32,1024]{1,0:T(8,128)(2,1)S(1)}, bf16[32,1024]{1,0:T(8,128)(2,1)S(1)}, u32[]{:S(2)}, u32[]{:S(2)}) collective-permute-start(bf16[32,1024]{1,0:T(8,128)(2,1)S(1)} %maximum_select_fusion.3), channel_id=1, source_target_pairs={{0,5},{5,0},{1,4},{4,1},{2,7},{7,2},{3,6},{6,3},{8,13},{13,8},{9,1... | collective-permute-start | bytes 196616 | tf_op jit(solution)/shard_map/ppermute | solution.py:316
  20.9 4.5 %shard_map.118.normed_hbm = bf16[1568,1024]{1,0:T(8,128)(2,1)} custom-call(bf16[1568,1024]{1,0:T(8,128)(2,1)} %tokens_ref.2), custom_call_target="tpu_custom_call" | custom-call | bytes 1024 | tf_op jit(solution)/shard_map/pallas_call | solution.py:111
  25.3 3.5 %shard_map.119.normed_ref = bf16[784,1024]{1,0:T(8,128)(2,1)} custom-call(bf16[784,1024]{1,0:T(8,128)(2,1)} %tokens_ref.1), custom_call_target="tpu_custom_call" | custom-call | bytes 1024 | tf_op jit(solution)/shard_map/pallas_call | solution.py:111
  28.9 13.3 %collective-permute-done.2 = bf16[32,1024]{1,0:T(8,128)(2,1)S(1)} collective-permute-done((bf16[32,1024]{1,0:T(8,128)(2,1)S(1)}, bf16[32,1024]{1,0:T(8,128)(2,1)S(1)}, u32[]{:S(2)}, u32[]{:S(2)}) %collective-permute-start.2) | collective-permute-done | bytes 65568 | tf_op jit(solution)/shard_map/ppermute | solution.py:316
  42.9 2.4 %shard_map.120 = bf16[16,64,1024]{2,1,0:T(8,128)(2,1)} custom-call(bf16[64,1024]{1,0:T(8,128)(2,1)} %maximum_select_fusion.block_ref), custom_call_target="tpu_custom_call" | custom-call | bytes 1024 | tf_op jit(solution)/shard_map/pallas_call | solution.py:93
  45.3 1.9 %all-to-all-done = bf16[32,32,1024]{2,1,0:T(8,128)(2,1)} async-done(((bf16[32,32,1024]{2,1,0:T(8,128)(2,1)}), bf16[32,32,1024]{2,1,0:T(8,128)(2,1)}, u32[]{:S(2)}, u32[]{:S(2)}) %all-to-all-start) | async-done | bytes 2097184 | tf_op jit(solution)/shard_map/all_to_all | solution.py:85
  47.2 1.7 %collective-permute-start.3 = (bf16[1024,1024]{1,0:T(8,128)(2,1)}, bf16[1024,1024]{1,0:T(8,128)(2,1)}, u32[]{:S(2)}, u32[]{:S(2)}) collective-permute-start(bf16[1024,1024]{1,0:T(8,128)(2,1)} %bitcast.weights_hbm.own_ref), channel_id=1, source_target_pairs={{0,2},{2,0},{1,3},{3,1},{4,6},{6,4},{5,7},{7,5},{8,10},{10,8},{9,1... | collective-permute-start | bytes 6291464 | tf_op jit(solution)/shard_map/ppermute | solution.py:59
  48.9 5.3 %all-to-all-start.2 = ((bf16[16,64,1024]{2,1,0:T(8,128)(2,1)}), bf16[16,64,1024]{2,1,0:T(8,128)(2,1)}, u32[]{:S(2)}, u32[]{:S(2)}) async-start(bf16[16,64,1024]{2,1,0:T(8,128)(2,1)} %shard_map.120), calls=%async_computation.2 | async-start | bytes 4194304 | tf_op jit(solution)/shard_map/all_to_all | solution.py:85
  54.2 12.7 %shard_map.122 = (bf16[1568,1024]{1,0:T(8,128)(2,1)}, bf16[256,1024]{1,0:T(8,128)(2,1)}, bf16[256,1024]{1,0:T(8,128)(2,1)}, bf16[256,1024]{1,0:T(8,128)(2,1)}, bf16[256,1024]{1,0:T(8,128)(2,1)}) custom-call(s32[1]{0:T(128)} %bitcast.1.which_ref.core_ref, bf16[1568,1024]{1,0:T(8,128)(2,1)} %shard_map.118.normed_hbm, ...), custom_call_target="tpu_custom_call" | custom-call | bytes 1024 | tf_op jit(solution)/shard_map/pallas_call | solution.py:234
  68.3 9.1 %shard_map.121.delta_hbm.delta_other_ref = bf16[1568,1024]{1,0:T(8,128)(2,1)} custom-call(s32[1]{0:T(128)S(6)} %sub.12.which_ref, bf16[1568,1024]{1,0:T(8,128)(2,1)} %shard_map.118.normed_hbm, bf16[1024,1024]{1,0:T(8,128)(2,1)} %collective-permute-done.3.weights_hbm.other_ref, bf16[1568,2048]{1,0:T(8,128)(2,1)} %cotangent_hbm.3), custom_call_target="tpu_custom_call" | custom-call | bytes 1024 | tf_op jit(solution)/shard_map/pallas_call | solution.py:234
  78.5 7.8 %shard_map.123 = bf16[1024,1024]{1,0:T(8,128)(2,1)} custom-call(bf16[1568,1024]{1,0:T(8,128)(2,1)} %shard_map.118.normed_hbm, bf16[1568,1024]{1,0:T(8,128)(2,1)} %shard_map.121.delta_hbm.delta_other_ref, bf16[256,1024]{1,0:T(8,128)(2,1)} %copy-done.2, bf16[256,1024]{1,0:T(8,128)(2,1)} %copy-done.3, bf16[256,1024]{1,0:T(8,128)(2,1)} %copy-done.4, ...), custom_call_target="tpu_custom_call" | custom-call | bytes 1024 | tf_op jit(solution)/shard_map/pallas_call | solution.py:234
  86.3 1.2 all-to-all-done.2
  87.6 1.1 collective-permute-start.8
  88.7 5.4 %all-to-all-start.1 = ((bf16[32,32,1024]{2,1,0:T(8,128)(2,1)}), bf16[32,32,1024]{2,1,0:T(8,128)(2,1)S(1)}, u32[]{:S(2)}, u32[]{:S(2)}) async-start(bf16[32,32,1024]{2,1,0:T(8,128)(2,1)} %bitcast.4), calls=%async_computation.1 | async-start | bytes 4194304 | tf_op jit(solution)/shard_map/all_to_all | solution.py:85
  94.2 14.3 %shard_map.125 = bf16[1568,1024]{1,0:T(8,128)(2,1)} custom-call(bf16[1568,1024]{1,0:T(8,128)(2,1)} %get-tuple-element.39.delta_own_ref, bf16[1568,1024]{1,0:T(8,128)(2,1)} %shard_map.121.delta_hbm.delta_other_ref, bf16[1024,1024]{1,0:T(8,128)(2,1)} %bitcast.weights_hbm.own_ref, bf16[1024,1024]{1,0:T(8,128)(2,1)} %collective-permute-done.3.weights_hbm.other_ref, ...), custom_call_target="tpu_custom_call" | custom-call | flops 6576668672 | tf_op jit(solution)/shard_map/pallas_call | solution.py:265
  108.5 8.2 %shard_map.124 = bf16[784,2048]{1,0:T(8,128)(2,1)} custom-call(s32[1]{0:T(128)} %bitcast.1.which_ref.core_ref, bf16[784,1024]{1,0:T(8,128)(2,1)} %shard_map.119.normed_ref, bf16[1024,1024]{1,0:T(8,128)(2,1)} %bitcast.3.own_ref, bf16[1024,1024]{1,0:T(8,128)(2,1)} %collective-permute-done.8.other_ref), custom_call_target="tpu_custom_call" | custom-call | flops 3288334336 | tf_op jit(solution)/shard_map/pallas_call | solution.py:291
  116.7 8.3 %all-to-all-done.1 = bf16[32,32,1024]{2,1,0:T(8,128)(2,1)S(1)} async-done(((bf16[32,32,1024]{2,1,0:T(8,128)(2,1)}), bf16[32,32,1024]{2,1,0:T(8,128)(2,1)S(1)}, u32[]{:S(2)}, u32[]{:S(2)}) %all-to-all-start.1) | async-done | bytes 2097184 | tf_op jit(solution)/shard_map/all_to_all | solution.py:85
  125.9 2.7 %collective-permute-start.10 = (bf16[16,1024]{1,0:T(8,128)(2,1)S(1)}, bf16[16,1024]{1,0:T(8,128)(2,1)S(1)}, u32[]{:S(2)}, u32[]{:S(2)}) collective-permute-start(bf16[16,1024]{1,0:T(8,128)(2,1)S(1)} %get-tuple-element.49), channel_id=1, source_target_pairs={{0,3},{1,2},{2,1},{3,0},{4,7},{5,6},{6,5},{7,4},{8,11},{9,10},{10,... | collective-permute-start | bytes 98312 | tf_op jit(solution)/shard_map/ppermute | solution.py:367
  128.6 2.3 %collective-permute-done.10 = bf16[16,1024]{1,0:T(8,128)(2,1)S(1)} collective-permute-done((bf16[16,1024]{1,0:T(8,128)(2,1)S(1)}, bf16[16,1024]{1,0:T(8,128)(2,1)S(1)}, u32[]{:S(2)}, u32[]{:S(2)}) %collective-permute-start.10) | collective-permute-done | bytes 32800 | tf_op jit(solution)/shard_map/ppermute | solution.py:367
  (41 shorter events, 6.5 us)
Async XLA Ops:
  1.6 2.4 %collective-permute-start = (bf16[16,1024]{1,0:T(8,128)(2,1)S(1)}, bf16[16,1024]{1,0:T(8,128)(2,1)S(1)}, u32[]{:S(2)}, u32[]{:S(2)}) collective-permute-start(bf16[16,1024]{1,0:T(8,128)(2,1)S(1)} %get-tuple-element.53), channel_id=1, source_target_pairs={{0,2},{2,0},{1,3},{3,1},{4,6},{6,4},{5,7},{7,5},{8,10},{10,8},{9,1... | collective-permute-start | bytes 98312 | tf_op jit(solution)/shard_map/ppermute | solution.py:59
  5.5 10.9 %copy-start.1 = (f32[16,2048]{1,0:T(8,128)S(1)}, f32[16,2048]{1,0:T(8,128)}, u32[]{:S(2)}) copy-start(f32[16,2048]{1,0:T(8,128)} %param.13) | copy-start | bytes 393220
  5.5 41.7 %all-to-all-start = ((bf16[32,32,1024]{2,1,0:T(8,128)(2,1)}), bf16[32,32,1024]{2,1,0:T(8,128)(2,1)}, u32[]{:S(2)}, u32[]{:S(2)}) async-start(bf16[32,32,1024]{2,1,0:T(8,128)(2,1)} %broadcast_in_dim.2), calls=%async_computation | async-start | bytes 4194304 | tf_op jit(solution)/shard_map/all_to_all | solution.py:85
  16.4 1.6 %collective-permute-start.1 = (bf16[16,1024]{1,0:T(8,128)(2,1)S(1)}, bf16[16,1024]{1,0:T(8,128)(2,1)S(1)}, u32[]{:S(2)}, u32[]{:S(2)}) collective-permute-start(bf16[16,1024]{1,0:T(8,128)(2,1)S(1)} %get-tuple-element.51), channel_id=1, source_target_pairs={{0,2},{2,0},{1,3},{3,1},{4,6},{6,4},{5,7},{7,5},{8,10},{10,8},{9,1... | collective-permute-start | bytes 98312 | tf_op jit(solution)/shard_map/ppermute | solution.py:59
  18.0 24.2 %collective-permute-start.2 = (bf16[32,1024]{1,0:T(8,128)(2,1)S(1)}, bf16[32,1024]{1,0:T(8,128)(2,1)S(1)}, u32[]{:S(2)}, u32[]{:S(2)}) collective-permute-start(bf16[32,1024]{1,0:T(8,128)(2,1)S(1)} %maximum_select_fusion.3), channel_id=1, source_target_pairs={{0,5},{5,0},{1,4},{4,1},{2,7},{7,2},{3,6},{6,3},{8,13},{13,8},{9,1... | collective-permute-start | bytes 196616 | tf_op jit(solution)/shard_map/ppermute | solution.py:316
  47.2 21.1 %collective-permute-start.3 = (bf16[1024,1024]{1,0:T(8,128)(2,1)}, bf16[1024,1024]{1,0:T(8,128)(2,1)}, u32[]{:S(2)}, u32[]{:S(2)}) collective-permute-start(bf16[1024,1024]{1,0:T(8,128)(2,1)} %bitcast.weights_hbm.own_ref), channel_id=1, source_target_pairs={{0,2},{2,0},{1,3},{3,1},{4,6},{6,4},{5,7},{7,5},{8,10},{10,8},{9,1... | collective-permute-start | bytes 6291464 | tf_op jit(solution)/shard_map/ppermute | solution.py:59
  48.9 38.7 %all-to-all-start.2 = ((bf16[16,64,1024]{2,1,0:T(8,128)(2,1)}), bf16[16,64,1024]{2,1,0:T(8,128)(2,1)}, u32[]{:S(2)}, u32[]{:S(2)}) async-start(bf16[16,64,1024]{2,1,0:T(8,128)(2,1)} %shard_map.120), calls=%async_computation.2 | async-start | bytes 4194304 | tf_op jit(solution)/shard_map/all_to_all | solution.py:85
  67.0 10.4 %collective-permute-start.4 = (bf16[256,1024]{1,0:T(8,128)(2,1)}, bf16[256,1024]{1,0:T(8,128)(2,1)S(1)}, u32[]{:S(2)}, u32[]{:S(2)}) collective-permute-start(bf16[256,1024]{1,0:T(8,128)(2,1)} %get-tuple-element.31), channel_id=1, source_target_pairs={{0,2},{2,0},{1,3},{3,1},{4,6},{6,4},{5,7},{7,5},{8,10},{10,8},{9,1... | collective-permute-start | bytes 1572872 | tf_op jit(solution)/shard_map/ppermute | solution.py:59
  67.5 9.9 %collective-permute-start.5 = (bf16[256,1024]{1,0:T(8,128)(2,1)}, bf16[256,1024]{1,0:T(8,128)(2,1)S(1)}, u32[]{:S(2)}, u32[]{:S(2)}) collective-permute-start(bf16[256,1024]{1,0:T(8,128)(2,1)} %get-tuple-element.32), channel_id=1, source_target_pairs={{0,2},{2,0},{1,3},{3,1},{4,6},{6,4},{5,7},{7,5},{8,10},{10,8},{9,1... | collective-permute-start | bytes 1572872 | tf_op jit(solution)/shard_map/ppermute | solution.py:59
  67.7 9.7 %collective-permute-start.6 = (bf16[256,1024]{1,0:T(8,128)(2,1)}, bf16[256,1024]{1,0:T(8,128)(2,1)S(1)}, u32[]{:S(2)}, u32[]{:S(2)}) collective-permute-start(bf16[256,1024]{1,0:T(8,128)(2,1)} %get-tuple-element.33), channel_id=1, source_target_pairs={{0,2},{2,0},{1,3},{3,1},{4,6},{6,4},{5,7},{7,5},{8,10},{10,8},{9,1... | collective-permute-start | bytes 1572872 | tf_op jit(solution)/shard_map/ppermute | solution.py:59
  68.1 9.4 %collective-permute-start.7 = (bf16[256,1024]{1,0:T(8,128)(2,1)}, bf16[256,1024]{1,0:T(8,128)(2,1)}, u32[]{:S(2)}, u32[]{:S(2)}) collective-permute-start(bf16[256,1024]{1,0:T(8,128)(2,1)} %get-tuple-element.34), channel_id=1, source_target_pairs={{0,2},{2,0},{1,3},{3,1},{4,6},{6,4},{5,7},{7,5},{8,10},{10,8},{9,1... | collective-permute-start | bytes 1572872 | tf_op jit(solution)/shard_map/ppermute | solution.py:59
  77.4 0.8 copy-start.2
  77.4 1.0 copy-start.3
  77.4 1.1 copy-start.4
  87.6 20.9 %collective-permute-start.8 = (bf16[1024,1024]{1,0:T(8,128)(2,1)}, bf16[1024,1024]{1,0:T(8,128)(2,1)}, u32[]{:S(2)}, u32[]{:S(2)}) collective-permute-start(bf16[1024,1024]{1,0:T(8,128)(2,1)} %bitcast.3.own_ref), channel_id=1, source_target_pairs={{0,2},{2,0},{1,3},{3,1},{4,6},{6,4},{5,7},{7,5},{8,10},{10,8},{9,1... | collective-permute-start | bytes 6291464 | tf_op jit(solution)/shard_map/ppermute | solution.py:59
  88.7 36.3 %all-to-all-start.1 = ((bf16[32,32,1024]{2,1,0:T(8,128)(2,1)}), bf16[32,32,1024]{2,1,0:T(8,128)(2,1)S(1)}, u32[]{:S(2)}, u32[]{:S(2)}) async-start(bf16[32,32,1024]{2,1,0:T(8,128)(2,1)} %bitcast.4), calls=%async_computation.1 | async-start | bytes 4194304 | tf_op jit(solution)/shard_map/all_to_all | solution.py:85
  116.7 14.3 %copy-start = (f32[16,2048]{1,0:T(8,128)S(1)}, f32[16,2048]{1,0:T(8,128)}, u32[]{:S(2)}) copy-start(f32[16,2048]{1,0:T(8,128)} %param.10) | copy-start | bytes 393220
  116.7 14.3 %copy-start.5 = (f32[16,2048]{1,0:T(8,128)S(1)}, f32[16,2048]{1,0:T(8,128)}, u32[]{:S(2)}) copy-start(f32[16,2048]{1,0:T(8,128)} %param.11) | copy-start | bytes 393220
  116.7 14.3 %copy-start.6 = (f32[16,2048]{1,0:T(8,128)S(1)}, f32[16,2048]{1,0:T(8,128)}, u32[]{:S(2)}) copy-start(f32[16,2048]{1,0:T(8,128)} %param.12) | copy-start | bytes 393220
  125.4 3.2 %collective-permute-start.11 = (bf16[16,1024]{1,0:T(8,128)(2,1)S(1)}, bf16[16,1024]{1,0:T(8,128)(2,1)S(1)}, u32[]{:S(2)}, u32[]{:S(2)}) collective-permute-start(bf16[16,1024]{1,0:T(8,128)(2,1)S(1)} %get-tuple-element.48), channel_id=1, source_target_pairs={{0,1},{1,0},{2,3},{3,2},{4,5},{5,4},{6,7},{7,6},{8,9},{9,8},{10,11... | collective-permute-start | bytes 98312 | tf_op jit(solution)/shard_map/ppermute | solution.py:366
  125.9 5.0 %collective-permute-start.10 = (bf16[16,1024]{1,0:T(8,128)(2,1)S(1)}, bf16[16,1024]{1,0:T(8,128)(2,1)S(1)}, u32[]{:S(2)}, u32[]{:S(2)}) collective-permute-start(bf16[16,1024]{1,0:T(8,128)(2,1)S(1)} %get-tuple-element.49), channel_id=1, source_target_pairs={{0,3},{1,2},{2,1},{3,0},{4,7},{5,6},{6,5},{7,4},{8,11},{9,10},{10,... | collective-permute-start | bytes 98312 | tf_op jit(solution)/shard_map/ppermute | solution.py:367
  128.6 2.3 %collective-permute-start.9 = (bf16[16,1024]{1,0:T(8,128)(2,1)S(1)}, bf16[16,1024]{1,0:T(8,128)(2,1)S(1)}, u32[]{:S(2)}, u32[]{:S(2)}) collective-permute-start(bf16[16,1024]{1,0:T(8,128)(2,1)S(1)} %get-tuple-element.49), channel_id=1, source_target_pairs={{0,2},{2,0},{1,3},{3,1},{4,6},{6,4},{5,7},{7,5},{8,10},{10,8},{9,1... | collective-permute-start | bytes 98312 | tf_op jit(solution)/shard_map/ppermute | solution.py:59

commit v5 on v4

--- a/solution.py
+++ b/solution.py
@@ -85,20 +85,36 @@
     return lax.all_to_all(blocks, chips, 0, 0, tiled=True)
 
 
-def copies_kernel(block_ref, copies_ref):
-    copies_ref[...] = jnp.broadcast_to(block_ref[...][None], copies_ref.shape)
-
-
-def copies_call(block, count, steps):
+def copies_kernel(place_ref, block_ref, beyond_ref, copies_hbm, whole_ref, sems):
+    first, size = place_ref[0] == 0, block_ref.shape[0]
+    mine, theirs = block_ref[...], beyond_ref[...]
+    whole_ref[:size, :] = jnp.where(first, mine, theirs)
+    whole_ref[size:, :] = jnp.where(first, theirs, mine)
+    out = [
+        pltpu.make_async_copy(whole_ref, copies_hbm.at[n], sems.at[n])
+        for n in range(copies_hbm.shape[0])
+    ]
+    for copy in out:
+        copy.start()
+    for copy in out:
+        copy.wait()
+
+
+def copies_call(place, block, beyond):
+    shape = (2 * block.shape[0], block.shape[1])
     return pl.pallas_call(
         copies_kernel,
-        grid=(steps,),
-        in_specs=[pl.BlockSpec(block.shape, lambda i: (0, 0))],
-        out_specs=pl.BlockSpec((count // steps,) + block.shape, lambda i: (i, 0, 0)),
-        out_shape=jax.ShapeDtypeStruct((count,) + block.shape, block.dtype),
+        in_specs=[
+            pl.BlockSpec(memory_space=pltpu.SMEM),
+            pl.BlockSpec(memory_space=pltpu.VMEM),
+            pl.BlockSpec(memory_space=pltpu.VMEM),
+        ],
+        out_specs=pl.BlockSpec(memory_space=pl.ANY),
+        out_shape=jax.ShapeDtypeStruct((16,) + shape, block.dtype),
+        scratch_shapes=[pltpu.VMEM(shape, block.dtype), pltpu.SemaphoreType.DMA((16,))],
         compiler_params=params(LIMIT),
         cost_estimate=cost(0, 1024),
-    )(block)
+    )(place.astype(jnp.int32).reshape(1), block, beyond)
 
 
 def norm_kernel(tokens_ref, normed_ref):
@@ -121,7 +137,7 @@
 
 LIMIT = 62
 TILES = ((0, 512), (512, 512), (1024, 544))
-PIECES = 4
+PIECES = 2
 
 
 def start_all(copies):
@@ -314,8 +330,7 @@
     weights_own = exchanged(copies).reshape(width, half)
     teacher_block = half_block(teacher_rows.astype(bf16), core)
     beyond = lax.ppermute(teacher_block, ("yh", "yl"), ACROSS)
-    teacher_block = in_order(teacher_block, beyond, "yh", 0)
-    teacher_copies = copies_call(teacher_block, 16, 1)
+    teacher_copies = copies_call(lax.axis_index("yh"), teacher_block, beyond)
     normed, teacher_normed = norm_call(tokens, 2), norm_call(global_tokens, 1)
     normed, teacher_normed, teacher_copies, weights_own = lax.optimization_barrier(
         (normed, teacher_normed, teacher_copies, weights_own)

time: 132 us -> 132 us (level)
    ppermute x1, starting transfers between devices: 2.7 us -> 0.93 us  [per_device(): lax.ppermute(other, ('core', 'yl'), [(0, 3), (1, 2), (2, 1), (3, 0)])]
    ppermute x9 -> x7, starting transfers between devices: 6.38 us -> 7.71 us  [swap(): return lax.ppermute(block, 'core', SWAP)]
  transfers between devices with their start and end apart: 15 -> 13, of which waited for: 7 -> 7; matrix products, arithmetic and copies ran while one was open for 1% -> 0% of each run, Pallas kernels for 47% -> 48%
where the time goes in v5:
time: 132 us; the launch traced here: 131 us
  Pallas kernels  62.7 us (48%)
  starting transfers between devices  33.1 us (25%)
  waiting for transfers between devices  29.3 us (22%)
  local copies, waits for them, and re-layouts  3.22 us (2%)
  other arithmetic  2.21 us (2%)
    pallas_call x3, Pallas kernels, local_call(): pl.pallas_call(kernel, in_specs=[pl.BlockSpec(memory_space=pltpu.SMEM) if...  29.9 us
    all_to_all x3, starting transfers between devices, exchanged(): return lax.all_to_all(blocks, chips, 0, 0, tiled=True)  21.1 us
    pallas_call x1, Pallas kernels, input_call(): pl.pallas_call(input_kernel, grid=(rows // 784,), in_specs=[deltas, delta...  14.3 us
    ppermute x1, waiting for transfers between devices, per_device(): beyond = lax.ppermute(teacher_block, ('yh', 'yl'), ACROSS)  13.3 us
    all_to_all x3, waiting for transfers between devices, exchanged(): return lax.all_to_all(blocks, chips, 0, 0, tiled=True)  11.9 us
    pallas_call x1, Pallas kernels, hidden_call(): pl.pallas_call(hidden_kernel, grid_spec=pltpu.PrefetchScalarGridSpec(num_...  8.22 us
    pallas_call x2, Pallas kernels, norm_call(): pl.pallas_call(norm_kernel, grid=(steps,), in_specs=[spec], out_specs=spe...  8 us
    ppermute x7, starting transfers between devices, swap(): return lax.ppermute(block, 'core', SWAP)  7.71 us
  transfers between devices with their start and end apart: 13, of which 7 were waited for; matrix products, arithmetic and copies ran while one was open for 0% of the time, Pallas kernels for 48%

profile of v5, /device:TPU:1, one launch (start us, length us, event | category | flops | bytes accessed | tf_op | source)
XLA Modules:
  0.0 131.4 jit_solution(6928388466453183612)
XLA Ops:
  1.6 1.5 %collective-permute-start = (bf16[16,1024]{1,0:T(8,128)(2,1)S(1)}, bf16[16,1024]{1,0:T(8,128)(2,1)S(1)}, u32[]{:S(2)}, u32[]{:S(2)}) collective-permute-start(bf16[16,1024]{1,0:T(8,128)(2,1)S(1)} %get-tuple-element.49), channel_id=1, source_target_pairs={{0,2},{2,0},{1,3},{3,1},{4,6},{6,4},{5,7},{7,5},{8,10},{10,8},{9,1... | collective-permute-start | bytes 98312 | tf_op jit(solution)/shard_map/ppermute | solution.py:59
  3.9 1.6 %broadcast_in_dim.2 = bf16[32,32,1024]{2,1,0:T(8,128)(2,1)} broadcast(bf16[32,1024]{1,0:T(8,128)(2,1)S(1)} %maximum_select_fusion.1), dimensions={1,2} | broadcast | bytes 2162688 | tf_op jit(solution)/shard_map/broadcast_in_dim | solution.py:81
  5.5 10.9 %all-to-all-start = ((bf16[32,32,1024]{2,1,0:T(8,128)(2,1)}), bf16[32,32,1024]{2,1,0:T(8,128)(2,1)}, u32[]{:S(2)}, u32[]{:S(2)}) async-start(bf16[32,32,1024]{2,1,0:T(8,128)(2,1)} %broadcast_in_dim.2), calls=%async_computation | async-start | bytes 4194304 | tf_op jit(solution)/shard_map/all_to_all | solution.py:85
  18.0 2.8 %collective-permute-start.2 = (bf16[32,1024]{1,0:T(8,128)(2,1)S(1)}, bf16[32,1024]{1,0:T(8,128)(2,1)S(1)}, u32[]{:S(2)}, u32[]{:S(2)}) collective-permute-start(bf16[32,1024]{1,0:T(8,128)(2,1)S(1)} %maximum_select_fusion.2.block_ref), channel_id=1, source_target_pairs={{0,5},{5,0},{1,4},{4,1},{2,7},{7,2},{3,6},{6,3},{8,13},{13,8},{9,1... | collective-permute-start | bytes 196616 | tf_op jit(solution)/shard_map/ppermute | solution.py:332
  20.9 4.5 %shard_map.118.normed_hbm = bf16[1568,1024]{1,0:T(8,128)(2,1)} custom-call(bf16[1568,1024]{1,0:T(8,128)(2,1)} %tokens_ref.2), custom_call_target="tpu_custom_call" | custom-call | bytes 1024 | tf_op jit(solution)/shard_map/pallas_call | solution.py:127
  25.4 3.5 %shard_map.119.normed_ref = bf16[784,1024]{1,0:T(8,128)(2,1)} custom-call(bf16[784,1024]{1,0:T(8,128)(2,1)} %tokens_ref.1), custom_call_target="tpu_custom_call" | custom-call | bytes 1024 | tf_op jit(solution)/shard_map/pallas_call | solution.py:127
  28.9 13.3 %collective-permute-done.2.beyond_ref = bf16[32,1024]{1,0:T(8,128)(2,1)S(1)} collective-permute-done((bf16[32,1024]{1,0:T(8,128)(2,1)S(1)}, bf16[32,1024]{1,0:T(8,128)(2,1)S(1)}, u32[]{:S(2)}, u32[]{:S(2)}) %collective-permute-start.2) | collective-permute-done | bytes 65568 | tf_op jit(solution)/shard_map/ppermute | solution.py:332
  42.8 2.3 %shard_map.120 = bf16[16,64,1024]{2,1,0:T(8,128)(2,1)} custom-call(s32[1]{0:T(128)} %bitcast.place_ref, bf16[32,1024]{1,0:T(8,128)(2,1)} %copy-done.3, bf16[32,1024]{1,0:T(8,128)(2,1)} %copy-done.6), custom_call_target="tpu_custom_call" | custom-call | bytes 1024 | tf_op jit(solution)/shard_map/pallas_call | solution.py:105
  45.2 2.0 %all-to-all-done = bf16[32,32,1024]{2,1,0:T(8,128)(2,1)} async-done(((bf16[32,32,1024]{2,1,0:T(8,128)(2,1)}), bf16[32,32,1024]{2,1,0:T(8,128)(2,1)}, u32[]{:S(2)}, u32[]{:S(2)}) %all-to-all-start) | async-done | bytes 2097184 | tf_op jit(solution)/shard_map/all_to_all | solution.py:85
  47.2 1.7 %collective-permute-start.3 = (bf16[1024,1024]{1,0:T(8,128)(2,1)}, bf16[1024,1024]{1,0:T(8,128)(2,1)}, u32[]{:S(2)}, u32[]{:S(2)}) collective-permute-start(bf16[1024,1024]{1,0:T(8,128)(2,1)} %bitcast.1.weights_hbm.own_ref), channel_id=1, source_target_pairs={{0,2},{2,0},{1,3},{3,1},{4,6},{6,4},{5,7},{7,5},{8,10},{10,8},{9,1... | collective-permute-start | bytes 6291464 | tf_op jit(solution)/shard_map/ppermute | solution.py:59
  48.9 5.3 %all-to-all-start.2 = ((bf16[16,64,1024]{2,1,0:T(8,128)(2,1)}), bf16[16,64,1024]{2,1,0:T(8,128)(2,1)}, u32[]{:S(2)}, u32[]{:S(2)}) async-start(bf16[16,64,1024]{2,1,0:T(8,128)(2,1)} %shard_map.120), calls=%async_computation.2 | async-start | bytes 4194304 | tf_op jit(solution)/shard_map/all_to_all | solution.py:85
  54.2 12.8 %shard_map.122 = (bf16[1568,1024]{1,0:T(8,128)(2,1)}, bf16[512,1024]{1,0:T(8,128)(2,1)}, bf16[512,1024]{1,0:T(8,128)(2,1)}) custom-call(s32[1]{0:T(128)} %bitcast.2.which_ref.core_ref, bf16[1568,1024]{1,0:T(8,128)(2,1)} %shard_map.118.normed_hbm, bf16[1024,1024]{1,0:T(8,128)(2,1)} %bitcast.1.weights_hbm.own_ref, bf16[1568,2048]{1,0:T(8,128)(2,1)} %cotangent_hbm.3), custom_call_target="tpu_custom_call" | custom-call | bytes 1024 | tf_op jit(solution)/shard_map/pallas_call | solution.py:250
  67.8 9.1 %shard_map.121.delta_hbm.delta_other_ref = bf16[1568,1024]{1,0:T(8,128)(2,1)} custom-call(s32[1]{0:T(128)S(6)} %sub.12.which_ref, bf16[1568,1024]{1,0:T(8,128)(2,1)} %shard_map.118.normed_hbm, bf16[1024,1024]{1,0:T(8,128)(2,1)} %collective-permute-done.3.weights_hbm.other_ref, bf16[1568,2048]{1,0:T(8,128)(2,1)} %cotangent_hbm.3), custom_call_target="tpu_custom_call" | custom-call | bytes 1024 | tf_op jit(solution)/shard_map/pallas_call | solution.py:250
  77.0 0.9 copy-done
  78.0 7.9 %shard_map.123 = bf16[1024,1024]{1,0:T(8,128)(2,1)} custom-call(bf16[1568,1024]{1,0:T(8,128)(2,1)} %shard_map.118.normed_hbm, bf16[1568,1024]{1,0:T(8,128)(2,1)} %shard_map.121.delta_hbm.delta_other_ref, bf16[512,1024]{1,0:T(8,128)(2,1)} %copy-done, bf16[512,1024]{1,0:T(8,128)(2,1)} %collective-permute-done.5.refs_1_), custom_call_target="tpu_custom_call" | custom-call | bytes 1024 | tf_op jit(solution)/shard_map/pallas_call | solution.py:250
  85.9 1.7 %all-to-all-done.2 = bf16[16,64,1024]{2,1,0:T(8,128)(2,1)} async-done(((bf16[16,64,1024]{2,1,0:T(8,128)(2,1)}), bf16[16,64,1024]{2,1,0:T(8,128)(2,1)}, u32[]{:S(2)}, u32[]{:S(2)}) %all-to-all-start.2) | async-done | bytes 2097184 | tf_op jit(solution)/shard_map/all_to_all | solution.py:85
  87.6 1.1 collective-permute-start.6
  88.7 4.9 %all-to-all-start.1 = ((bf16[32,32,1024]{2,1,0:T(8,128)(2,1)}), bf16[32,32,1024]{2,1,0:T(8,128)(2,1)S(1)}, u32[]{:S(2)}, u32[]{:S(2)}) async-start(bf16[32,32,1024]{2,1,0:T(8,128)(2,1)} %bitcast.5), calls=%async_computation.1 | async-start | bytes 4194304 | tf_op jit(solution)/shard_map/all_to_all | solution.py:85
  93.7 14.3 %shard_map.125 = bf16[1568,1024]{1,0:T(8,128)(2,1)} custom-call(bf16[1568,1024]{1,0:T(8,128)(2,1)} %get-tuple-element.35.delta_own_ref, bf16[1568,1024]{1,0:T(8,128)(2,1)} %shard_map.121.delta_hbm.delta_other_ref, bf16[1024,1024]{1,0:T(8,128)(2,1)} %bitcast.1.weights_hbm.own_ref, bf16[1024,1024]{1,0:T(8,128)(2,1)} %collective-permute-done.3.weights_hbm.other_ref, ...), custom_call_target="tpu_custom_call" | custom-call | flops 6576668672 | tf_op jit(solution)/shard_map/pallas_call | solution.py:281
  108.0 8.2 %shard_map.124 = bf16[784,2048]{1,0:T(8,128)(2,1)} custom-call(s32[1]{0:T(128)} %bitcast.2.which_ref.core_ref, bf16[784,1024]{1,0:T(8,128)(2,1)} %shard_map.119.normed_ref, bf16[1024,1024]{1,0:T(8,128)(2,1)} %bitcast.4.own_ref, bf16[1024,1024]{1,0:T(8,128)(2,1)} %collective-permute-done.6.other_ref), custom_call_target="tpu_custom_call" | custom-call | flops 3288334336 | tf_op jit(solution)/shard_map/pallas_call | solution.py:307
  116.2 8.2 %all-to-all-done.1 = bf16[32,32,1024]{2,1,0:T(8,128)(2,1)S(1)} async-done(((bf16[32,32,1024]{2,1,0:T(8,128)(2,1)}), bf16[32,32,1024]{2,1,0:T(8,128)(2,1)S(1)}, u32[]{:S(2)}, u32[]{:S(2)}) %all-to-all-start.1) | async-done | bytes 2097184 | tf_op jit(solution)/shard_map/all_to_all | solution.py:85
  125.3 1.8 %collective-permute-start.7 = (bf16[16,1024]{1,0:T(8,128)(2,1)S(1)}, bf16[16,1024]{1,0:T(8,128)(2,1)S(1)}, u32[]{:S(2)}, u32[]{:S(2)}) collective-permute-start(bf16[16,1024]{1,0:T(8,128)(2,1)S(1)} %get-tuple-element.45), channel_id=1, source_target_pairs={{0,2},{2,0},{1,3},{3,1},{4,6},{6,4},{5,7},{7,5},{8,10},{10,8},{9,1... | collective-permute-start | bytes 98312 | tf_op jit(solution)/shard_map/ppermute | solution.py:59
  127.1 0.9 collective-permute-start.8
  128.1 2.4 %collective-permute-done.8 = bf16[16,1024]{1,0:T(8,128)(2,1)S(1)} collective-permute-done((bf16[16,1024]{1,0:T(8,128)(2,1)S(1)}, bf16[16,1024]{1,0:T(8,128)(2,1)S(1)}, u32[]{:S(2)}, u32[]{:S(2)}) %collective-permute-start.8) | collective-permute-done | bytes 32800 | tf_op jit(solution)/shard_map/ppermute | solution.py:382
  (36 shorter events, 6.6 us)
Async XLA Ops:
  1.6 2.4 %collective-permute-start = (bf16[16,1024]{1,0:T(8,128)(2,1)S(1)}, bf16[16,1024]{1,0:T(8,128)(2,1)S(1)}, u32[]{:S(2)}, u32[]{:S(2)}) collective-permute-start(bf16[16,1024]{1,0:T(8,128)(2,1)S(1)} %get-tuple-element.49), channel_id=1, source_target_pairs={{0,2},{2,0},{1,3},{3,1},{4,6},{6,4},{5,7},{7,5},{8,10},{10,8},{9,1... | collective-permute-start | bytes 98312 | tf_op jit(solution)/shard_map/ppermute | solution.py:59
  5.5 10.9 %copy-start.2 = (f32[16,2048]{1,0:T(8,128)S(1)}, f32[16,2048]{1,0:T(8,128)}, u32[]{:S(2)}) copy-start(f32[16,2048]{1,0:T(8,128)} %param.13) | copy-start | bytes 393220
  5.5 41.7 %all-to-all-start = ((bf16[32,32,1024]{2,1,0:T(8,128)(2,1)}), bf16[32,32,1024]{2,1,0:T(8,128)(2,1)}, u32[]{:S(2)}, u32[]{:S(2)}) async-start(bf16[32,32,1024]{2,1,0:T(8,128)(2,1)} %broadcast_in_dim.2), calls=%async_computation | async-start | bytes 4194304 | tf_op jit(solution)/shard_map/all_to_all | solution.py:85
  16.4 1.6 %collective-permute-start.1 = (bf16[16,1024]{1,0:T(8,128)(2,1)S(1)}, bf16[16,1024]{1,0:T(8,128)(2,1)S(1)}, u32[]{:S(2)}, u32[]{:S(2)}) collective-permute-start(bf16[16,1024]{1,0:T(8,128)(2,1)S(1)} %get-tuple-element.47), channel_id=1, source_target_pairs={{0,2},{2,0},{1,3},{3,1},{4,6},{6,4},{5,7},{7,5},{8,10},{10,8},{9,1... | collective-permute-start | bytes 98312 | tf_op jit(solution)/shard_map/ppermute | solution.py:59
  18.0 7.3 %copy-start.3 = (bf16[32,1024]{1,0:T(8,128)(2,1)}, bf16[32,1024]{1,0:T(8,128)(2,1)S(1)}, u32[]{:S(2)}) copy-start(bf16[32,1024]{1,0:T(8,128)(2,1)S(1)} %maximum_select_fusion.2.block_ref) | copy-start | bytes 196612
  18.0 24.1 %collective-permute-start.2 = (bf16[32,1024]{1,0:T(8,128)(2,1)S(1)}, bf16[32,1024]{1,0:T(8,128)(2,1)S(1)}, u32[]{:S(2)}, u32[]{:S(2)}) collective-permute-start(bf16[32,1024]{1,0:T(8,128)(2,1)S(1)} %maximum_select_fusion.2.block_ref), channel_id=1, source_target_pairs={{0,5},{5,0},{1,4},{4,1},{2,7},{7,2},{3,6},{6,3},{8,13},{13,8},{9,1... | collective-permute-start | bytes 196616 | tf_op jit(solution)/shard_map/ppermute | solution.py:332
  42.2 0.6 copy-start.6
  47.2 20.7 %collective-permute-start.3 = (bf16[1024,1024]{1,0:T(8,128)(2,1)}, bf16[1024,1024]{1,0:T(8,128)(2,1)}, u32[]{:S(2)}, u32[]{:S(2)}) collective-permute-start(bf16[1024,1024]{1,0:T(8,128)(2,1)} %bitcast.1.weights_hbm.own_ref), channel_id=1, source_target_pairs={{0,2},{2,0},{1,3},{3,1},{4,6},{6,4},{5,7},{7,5},{8,10},{10,8},{9,1... | collective-permute-start | bytes 6291464 | tf_op jit(solution)/shard_map/ppermute | solution.py:59
  48.9 38.6 %all-to-all-start.2 = ((bf16[16,64,1024]{2,1,0:T(8,128)(2,1)}), bf16[16,64,1024]{2,1,0:T(8,128)(2,1)}, u32[]{:S(2)}, u32[]{:S(2)}) async-start(bf16[16,64,1024]{2,1,0:T(8,128)(2,1)} %shard_map.120), calls=%async_computation.2 | async-start | bytes 4194304 | tf_op jit(solution)/shard_map/all_to_all | solution.py:85
  67.1 9.9 %collective-permute-start.4 = (bf16[512,1024]{1,0:T(8,128)(2,1)}, bf16[512,1024]{1,0:T(8,128)(2,1)S(1)}, u32[]{:S(2)}, u32[]{:S(2)}) collective-permute-start(bf16[512,1024]{1,0:T(8,128)(2,1)} %get-tuple-element.29), channel_id=1, source_target_pairs={{0,2},{2,0},{1,3},{3,1},{4,6},{6,4},{5,7},{7,5},{8,10},{10,8},{9,1... | collective-permute-start | bytes 3145736 | tf_op jit(solution)/shard_map/ppermute | solution.py:59
  67.6 9.3 %collective-permute-start.5 = (bf16[512,1024]{1,0:T(8,128)(2,1)}, bf16[512,1024]{1,0:T(8,128)(2,1)}, u32[]{:S(2)}, u32[]{:S(2)}) collective-permute-start(bf16[512,1024]{1,0:T(8,128)(2,1)} %get-tuple-element.30), channel_id=1, source_target_pairs={{0,2},{2,0},{1,3},{3,1},{4,6},{6,4},{5,7},{7,5},{8,10},{10,8},{9,1... | collective-permute-start | bytes 3145736 | tf_op jit(solution)/shard_map/ppermute | solution.py:59
  77.0 1.0 copy-start
  87.6 20.4 %collective-permute-start.6 = (bf16[1024,1024]{1,0:T(8,128)(2,1)}, bf16[1024,1024]{1,0:T(8,128)(2,1)}, u32[]{:S(2)}, u32[]{:S(2)}) collective-permute-start(bf16[1024,1024]{1,0:T(8,128)(2,1)} %bitcast.4.own_ref), channel_id=1, source_target_pairs={{0,2},{2,0},{1,3},{3,1},{4,6},{6,4},{5,7},{7,5},{8,10},{10,8},{9,1... | collective-permute-start | bytes 6291464 | tf_op jit(solution)/shard_map/ppermute | solution.py:59
  88.7 35.7 %all-to-all-start.1 = ((bf16[32,32,1024]{2,1,0:T(8,128)(2,1)}), bf16[32,32,1024]{2,1,0:T(8,128)(2,1)S(1)}, u32[]{:S(2)}, u32[]{:S(2)}) async-start(bf16[32,32,1024]{2,1,0:T(8,128)(2,1)} %bitcast.5), calls=%async_computation.1 | async-start | bytes 4194304 | tf_op jit(solution)/shard_map/all_to_all | solution.py:85
  116.2 14.3 %copy-start.1 = (f32[16,2048]{1,0:T(8,128)S(1)}, f32[16,2048]{1,0:T(8,128)}, u32[]{:S(2)}) copy-start(f32[16,2048]{1,0:T(8,128)} %param.10) | copy-start | bytes 393220
  116.2 14.3 %copy-start.4 = (f32[16,2048]{1,0:T(8,128)S(1)}, f32[16,2048]{1,0:T(8,128)}, u32[]{:S(2)}) copy-start(f32[16,2048]{1,0:T(8,128)} %param.11) | copy-start | bytes 393220
  116.2 14.3 %copy-start.5 = (f32[16,2048]{1,0:T(8,128)S(1)}, f32[16,2048]{1,0:T(8,128)}, u32[]{:S(2)}) copy-start(f32[16,2048]{1,0:T(8,128)} %param.12) | copy-start | bytes 393220
  124.8 3.3 %collective-permute-start.9 = (bf16[16,1024]{1,0:T(8,128)(2,1)S(1)}, bf16[16,1024]{1,0:T(8,128)(2,1)S(1)}, u32[]{:S(2)}, u32[]{:S(2)}) collective-permute-start(bf16[16,1024]{1,0:T(8,128)(2,1)S(1)} %get-tuple-element.44), channel_id=1, source_target_pairs={{0,1},{1,0},{2,3},{3,2},{4,5},{5,4},{6,7},{7,6},{8,9},{9,8},{10,11... | collective-permute-start | bytes 98312 | tf_op jit(solution)/shard_map/ppermute | solution.py:381
  125.3 2.8 %collective-permute-start.7 = (bf16[16,1024]{1,0:T(8,128)(2,1)S(1)}, bf16[16,1024]{1,0:T(8,128)(2,1)S(1)}, u32[]{:S(2)}, u32[]{:S(2)}) collective-permute-start(bf16[16,1024]{1,0:T(8,128)(2,1)S(1)} %get-tuple-element.45), channel_id=1, source_target_pairs={{0,2},{2,0},{1,3},{3,1},{4,6},{6,4},{5,7},{7,5},{8,10},{10,8},{9,1... | collective-permute-start | bytes 98312 | tf_op jit(solution)/shard_map/ppermute | solution.py:59
  127.1 3.3 %collective-permute-start.8 = (bf16[16,1024]{1,0:T(8,128)(2,1)S(1)}, bf16[16,1024]{1,0:T(8,128)(2,1)S(1)}, u32[]{:S(2)}, u32[]{:S(2)}) collective-permute-start(bf16[16,1024]{1,0:T(8,128)(2,1)S(1)} %get-tuple-element.45), channel_id=1, source_target_pairs={{0,3},{1,2},{2,1},{3,0},{4,7},{5,6},{6,5},{7,4},{8,11},{9,10},{10,... | collective-permute-start | bytes 98312 | tf_op jit(solution)/shard_map/ppermute | solution.py:382
